TPU v7x, 32 devices: a whole 2x2x4 slice. The times are simulated.
32 devices in a mesh: dp: 2 (over y), owner: 16 (over z, x, core).
Axes of the slice: x: 2, y: 2, z: 4, core: 2. Of those that a mesh axis runs over, the one named last changes fastest.
Arguments:
- partials: bfloat16 [32, 48, 128, 128], P(('dp', 'owner')), may hold values from -1.25 to 1.25
- owners: int32 [48], replicated, may hold values from 0 to 15, as said below
- step_count: int32 [1], replicated, may hold values from 1 to 49
- master: float32 [96, 128, 128], P('owner'), may hold values from -0.3125 to 0.3125
- moment: float32 [96, 128, 128], P('owner'), may hold values from -4 to 4
- second: float32 [96, 128, 128], P('owner'), may hold values from 0.1 to 10
- stat_left: float32 [96, 128, 128], P('owner'), may hold values from -1.5 to 82
- stat_right: float32 [96, 128, 128], P('owner'), may hold values from -1.5 to 82
- basis_left: float32 [96, 128, 128], P('owner'), may hold values from -0.12 to 1.12
- basis_right: float32 [96, 128, 128], P('owner'), may hold values from -0.12 to 1.12
Outputs:
- weights_all: bfloat16 [48, 128, 128], replicated
- direction: float32 [96, 128, 128], P('owner')
- left_new: float32 [96, 128, 128], P('owner')
- right_new: float32 [96, 128, 128], P('owner')
Inputs may be any that keep to these rules, and one draw needn't show every extreme that they name: `owners`: each owner index is named by at least one and at most 6 blocks, and some index by exactly 6.
All inputs are finite; a program needn't handle non-finite values.
Results may differ from a plain program's by a relative error of at most 0.0065.
Values may be sent and summed in bfloat16 or wider, within the bound.
No kernel may reach another device: no remote copies, remote signals or barrier semaphores. Data moves between devices by JAX's collectives and lax.ppermute only.
A program may use at most 128 MiB of HBM per device.

v0:
```python
import functools
import math

import jax
import jax.numpy as jnp
from jax import lax
from jax.experimental import pallas as pl
from jax.experimental.pallas import tpu as pltpu
from jax.sharding import PartitionSpec as P

NS_ITERS = 6
AXES = ("dp", "owner")
F32 = jnp.float32
BF16 = jnp.bfloat16
VMEM_LIMIT = 48 * 1024 * 1024
VMEM = pl.BlockSpec(memory_space=pltpu.VMEM)
SMEM = pl.BlockSpec(memory_space=pltpu.SMEM)
HBM = pl.BlockSpec(memory_space=pltpu.HBM)


def shape(dims, dtype):
    return jax.ShapeDtypeStruct(dims, dtype)


class Chain:
    def __init__(self):
        self.token = None

    def call(self, kernel, scalars, arrays, outs, flops=0, scratch=(), specs=None, moved=0, reuse=()):
        moved = moved or sum(math.prod(a.shape) * a.dtype.itemsize for a in [*arrays, *outs])
        count = len(scalars) + len(arrays)
        tokens = () if self.token is None else (self.token,)
        kept = count + len(tokens)
        count_in = kept + len(reuse)
        specs = specs or [VMEM] * len(outs)

        def run(*refs):
            refs = list(refs)
            token = refs.pop(count_in + len(outs))
            kernel(*refs[:count], *refs[count_in:])
            token[...] = jnp.zeros_like(token)

        *results, self.token = pl.pallas_call(
            run,
            out_shape=(*outs, shape((8, 128), F32)),
            in_specs=[SMEM] * len(scalars)
            + [VMEM] * len(arrays)
            + [VMEM] * len(tokens)
            + [HBM] * len(reuse),
            out_specs=(*specs, VMEM),
            scratch_shapes=list(scratch),
            input_output_aliases={kept + index: index for index in range(len(reuse))},
            compiler_params=pltpu.CompilerParams(vmem_limit_bytes=VMEM_LIMIT),
            cost_estimate=pl.CostEstimate(flops=flops, bytes_accessed=moved, transcendentals=0),
        )(*(pltpu.with_memory_space_constraint(a, pltpu.SMEM) for a in scalars), *arrays, *tokens, *reuse)
        return results


class Grid:
    def __init__(self, dp_count, owner_count):
        self.dp, self.core = dp_count, 2
        self.high = 4
        self.middle = owner_count // (self.core * self.high)
        self.owners = owner_count

    def place(self):
        owner = lax.axis_index("owner")
        high, rest = lax.div(owner, self.core * self.middle), lax.rem(owner, self.core * self.middle)
        return lax.axis_index("dp"), high, lax.div(rest, self.core), lax.rem(rest, self.core)

    def swap(self, array, dp=0, high=0, middle=0, core=0):
        step = (high * self.middle + middle) * self.core + core
        pairs = [
            (d * self.owners + o, (d ^ dp) * self.owners + (o ^ step))
            for d in range(self.dp)
            for o in range(self.owners)
        ]
        return lax.ppermute(array, AXES, pairs)


def split(value):
    top = value.astype(BF16)
    return top, (value - top.astype(F32)).astype(BF16)


def dot(left, right, dims):
    return lax.dot_general(left, right, (dims, ((), ())), preferred_element_type=F32)


NN = ((1,), (0,))
NT = ((1,), (1,))
TN = ((0,), (0,))


def as_left(value, axis=1):
    return jnp.concatenate(split(value), axis)


def as_right(value):
    half = jnp.concatenate(split(value), 1)
    return jnp.concatenate([half, half], 0)


def product(left, right, dims=NN):
    wide = dot(left, right, dims)
    size = wide.shape[1] // 2
    return wide[:, :size] + wide[:, size:]


def log2(count):
    return count.bit_length() - 1


class Table:
    def __init__(self, grid, slots):
        self.columns = grid.middle * grid.core
        self.groups = math.gcd(slots, grid.dp)
        self.shares = grid.dp // self.groups
        self.each = slots // self.groups
        self.length = grid.high * self.each
        self.rooms = (self.length * 2 // 3, self.length * 3 // 4, self.length)
        self.listed = 0
        self.counts = self.columns * self.groups * self.length
        self.inverse = self.counts + self.columns * self.groups
        self.held = self.inverse + self.length
        self.place = self.held + 1
        self.size = self.place + 4

    def slot(self, info, group, index):
        turn = group + self.groups - lax.rem(info[self.place + 1], self.groups)
        return self.groups * index + lax.rem(turn, self.groups)


def table_kernel(grid, table, owners, source, out, level, fetched, seen, sem):
    copy = pltpu.make_async_copy(source, fetched, sem)
    copy.start()
    place = grid.place()
    for owner in range(grid.owners):
        seen[owner] = 0
    for part in range(table.columns * table.groups):
        out[table.counts + part] = 0
    for at in range(table.length):
        out[table.inverse + at] = -1
    column_mine = place[2] * grid.core + place[3]
    mine = column_mine * table.groups + lax.div(place[0], table.shares)

    def step(block, carry):
        owner = owners[block]
        rank = seen[owner]
        seen[owner] = rank + 1
        column, high = owner & (table.columns - 1), owner >> log2(table.columns)
        group, index = (rank + high) & (table.groups - 1), rank >> log2(table.groups)
        part = column * table.groups + group
        at = out[table.counts + part]
        out[table.counts + part] = at + 1
        out[table.listed + part * table.length + at] = block

        @pl.when(part == mine)
        def _():
            out[table.inverse + high * table.each + index] = at

        return carry

    lax.fori_loop(0, owners.shape[0], step, 0, unroll=8)
    out[table.held] = seen[place[1] * table.columns + column_mine]
    most = out[table.counts]
    for part in range(1, table.columns * table.groups):
        most = jnp.maximum(most, out[table.counts + part])
    level[0] = sum((most > room).astype(jnp.int32) for room in table.rooms[:-1])
    for at in range(4):
        out[table.place + at] = place[at]
    copy.wait()


def part_of(grid, table, info, dc, dm, dd):
    column = (info[table.place + 2] ^ dm) * grid.core + (info[table.place + 3] ^ dc)
    dp = info[table.place] ^ dd
    part = column * table.groups + lax.div(dp, table.shares)
    return info[table.counts + part], table.listed + part * table.length, lax.rem(dp, table.shares)


def copy_kernel(source, out):
    out[...] = source[...]


def spread_kernel(grid, table, cuts, info, own, other, *outs):
    rows = own.shape[1] // table.shares
    pieces = len(cuts) - 1
    for index in range(grid.middle * grid.dp):
        count, first, share = part_of(grid, table, info, 0, index // grid.dp, index % grid.dp)
        part = pl.ds(pl.multiple_of(share * rows, rows), rows)
        for piece in range(pieces):
            out = outs[index * pieces + piece]

            def put(at, carry):
                block = info[first + at]
                total = own[block, part].astype(F32) + other[block, part].astype(F32)
                out[at - cuts[piece]] = total.astype(BF16)
                return carry

            lax.fori_loop(cuts[piece], jnp.minimum(count, cuts[piece + 1]), put, 0)


def total_of(arrays, at):
    total = arrays[0][at].astype(F32)
    for array in arrays[1:]:
        total = total + array[at].astype(F32)
    return total.astype(BF16)


def gather_sum_kernel(grid, table, cuts, info, *refs):
    arrays, outs, every = refs[: -1 - grid.high], refs[-1 - grid.high : -1], refs[-1]
    each = len(arrays) // (len(cuts) - 1)
    for piece, (begin, end) in enumerate(zip(cuts, cuts[1:])):
        for at in range(begin, end):
            every[at] = total_of(arrays[piece * each : (piece + 1) * each], at - begin)
    for dh in range(grid.high):
        first = table.inverse + (info[table.place + 1] ^ dh) * table.each
        for index in range(table.each):
            outs[dh][index] = every[jnp.clip(info[first + index], 0, cuts[-1] - 1)]


def merge_kernel(*refs):
    count = len(refs) // 3
    for one, two, out in zip(refs[:count], refs[count : 2 * count], refs[2 * count :], strict=True):
        for at in range(out.shape[0]):
            out[at] = total_of((one, two), at)


def sum_kernel(*refs):
    arrays, out = refs[:-1], refs[-1]
    for slot in range(out.shape[0]):
        out[slot] = total_of(arrays, slot)


def prepare_kernel(moment, left, right, rot_old, left_plain, left_turned, right_tall, right_turned):
    for slot in range(rot_old.shape[0]):
        left_t, right_t = left[slot].T, right[slot].T
        half = product(as_left(moment[slot]), as_right(right[slot]))
        left_turned[slot] = as_left(left_t)
        rot_old[slot] = product(as_left(left_t), as_right(half))
        left_plain[slot] = as_left(left[slot])
        right_tall[slot] = as_left(right[slot], 0)
        right_turned[slot] = as_right(right_t)


def rotate(gradient, rot_old, second, left_turned, right_tall, right_turned, c, pairs):
    halves = [dot(jnp.concatenate([gradient[i]] * 2, 1), right_tall[slot], NN) for i, slot in pairs]
    rotated = [
        product(left_turned[slot], as_right(half)) for half, (_, slot) in zip(halves, pairs, strict=True)
    ]
    turned = []
    for value, (_, slot) in zip(rotated, pairs, strict=True):
        rot_moment = 0.95 * rot_old[slot] + 0.05 * value
        second_new = 0.95 * second[slot] + 0.05 * value * value
        scaled = rot_moment / c / (jnp.sqrt(second_new / c) + 1e-08)
        turned.append(product(as_left(scaled), right_turned[slot]))
    return turned


def step_kernel(grid, table, info, correction, *refs):
    parts = refs[: table.shares]
    (rot_old, second, master, left_plain, left_turned, right_tall, right_turned) = refs[table.shares : -3]
    gradient, turned, updated = refs[-3:]
    rows = parts[0].shape[1]
    dp = info[table.place]
    group, share = lax.div(dp, table.shares), lax.rem(dp, table.shares)
    for dd in range(table.shares):
        gradient[:, pl.ds(pl.multiple_of((share ^ dd) * rows, rows), rows), :] = parts[dd][...]
    mine = pl.ds(pl.multiple_of(share * rows, rows), rows)
    pairs = [(index, table.slot(info, group, index)) for index in range(table.each)]
    values = rotate(
        gradient, rot_old, second, left_turned, right_tall, right_turned, correction[0], pairs
    )
    for value, (index, slot) in zip(values, pairs, strict=True):
        turned[index] = value
        weights = master[slot, mine]
        moved = product(left_plain[slot, mine], as_right(value))
        moved = jnp.where(slot < info[table.held], moved, 0.0)
        updated[index] = (weights - 0.01 * (moved + 0.1 * weights)).astype(BF16)


def refresh(gradient, left_stat, right_stat, left, right, pairs):
    iterates = []
    for dims, stat, basis in ((NT, left_stat, left), (TN, right_stat, right)):
        for index, slot in pairs:
            gram = dot(gradient[index], gradient[index], dims)
            power = product(as_left(0.95 * stat[slot] + 0.05 * gram), as_right(basis[slot]))
            iterates.append(power / (jnp.sqrt(jnp.sum(power * power)) + 1e-06))
    for _ in range(NS_ITERS):
        squares = [product(as_left(x, 0), as_right(x), TN) for x in iterates]
        iterates = [
            1.5 * x - 0.5 * product(as_left(x), as_right(square))
            for x, square in zip(iterates, squares, strict=True)
        ]
    return iterates[: len(pairs)], iterates[len(pairs) :]


def own_kernel(table, info, gradient, turned, left_plain, stat_left, stat_right, left, right, *refs):
    outs, (held, sem) = refs[:3], refs[3:]
    group = lax.div(info[table.place], table.shares)
    pairs = [(index, table.slot(info, group, index)) for index in range(table.each)]
    new_left, new_right = refresh(gradient, stat_left, stat_right, left, right, pairs)
    copies = []
    for index, slot in pairs:
        live = slot < info[table.held]
        moved = product(left_plain[slot], as_right(turned[index]))
        held[0, index] = jnp.where(live, moved, 0.0)
        held[1, index] = jnp.where(live, new_left[index], left[slot])
        held[2, index] = jnp.where(live, new_right[index], right[slot])
        copies += [pltpu.make_async_copy(held.at[n, index], outs[n].at[slot], sem) for n in range(3)]
    for copy in copies:
        copy.start()
    for copy in copies:
        copy.wait()


def others_kernel(table, info, *refs):
    count = table.groups - 1
    gradients, bases, (left_out, right_out) = refs[:count], refs[count : count + 4], refs[-2:]
    group = lax.div(info[table.place], table.shares)
    for dg, gradient in enumerate(gradients, 1):
        pairs = [(index, table.slot(info, group ^ dg, index)) for index in range(table.each)]
        new_left, new_right = refresh(gradient, *bases, pairs)
        for index, slot in pairs:
            at = (dg - 1) * table.each + index
            live = slot < info[table.held]
            left_out[at] = jnp.where(live, new_left[index], bases[2][slot])
            right_out[at] = jnp.where(live, new_right[index], bases[3][slot])


def finish_kernel(grid, table, layout, info, correction, *refs):
    count = table.groups - 1
    gradients, refs = refs[:count], refs[count:]
    (rot_old, second, left_plain, left_turned, right_tall, right_turned) = refs[:6]
    new_left, new_right, *packed = refs[6 : 8 + len(layout)]
    direction, left_out, right_out, weights, held, sem = refs[8 + len(layout) :]
    place_blocks(grid, table, layout, 0, info, packed, weights, sem, lambda copy: copy.start())
    group = lax.div(info[table.place], table.shares)
    every = [
        (dg, index, table.slot(info, group ^ dg, index))
        for dg in range(1, table.groups)
        for index in range(table.each)
    ]
    copies = []
    for at, (_, _, slot) in enumerate(every):
        copies.append(pltpu.make_async_copy(new_left.at[at], left_out.at[slot], sem))
        copies.append(pltpu.make_async_copy(new_right.at[at], right_out.at[slot], sem))
    for copy in copies:
        copy.start()
    for dg, gradient in enumerate(gradients, 1):
        pairs = [(index, slot) for owner, index, slot in every if owner == dg]
        turned = rotate(
            gradient, rot_old, second, left_turned, right_tall, right_turned, correction[0], pairs
        )
        for index, slot in pairs:
            moved = product(left_plain[slot], as_right(turned[index]))
            at = (dg - 1) * table.each + index
            held[at] = jnp.where(slot < info[table.held], moved, 0.0)
            copies.append(pltpu.make_async_copy(held.at[at], direction.at[slot], sem))
            copies[-1].start()
    for copy in copies:
        copy.wait()
    place_blocks(grid, table, layout, 0, info, packed, weights, sem, lambda copy: copy.wait())


def join_kernel(grid, table, cuts, info, *refs):
    pieces = len(cuts) - 1
    arrays, outs, every = refs[: grid.high], refs[-1 - pieces : -1], refs[-1]
    spare = info[table.counts + part_index(grid, table, info)]
    for dh in range(grid.high):
        first = table.inverse + (info[table.place + 1] ^ dh) * table.each
        for index in range(table.each):
            at = info[first + index]
            every[jnp.where(at < 0, spare, at)] = arrays[dh][index]
            spare = spare + (at < 0).astype(jnp.int32)
    for out, begin, end in zip(outs, cuts, cuts[1:]):
        out[...] = every[begin:end]


def pack_kernel(*refs):
    arrays, out = refs[:-1], refs[-1]
    begin = 0
    for array in arrays:
        out[begin : begin + array.shape[0]] = array[...]
        begin += array.shape[0]


def part_index(grid, table, info):
    column = info[table.place + 2] * grid.core + info[table.place + 3]
    return column * table.groups + lax.div(info[table.place], table.shares)


def place_blocks(grid, table, layout, core, info, packed, out, sem, act):
    rows = out.shape[1] // table.shares
    for array, pieces in zip(packed, layout, strict=True):
        base = 0
        for (dm, dd), begin, end in pieces:
            count, first, share = part_of(grid, table, info, core, dm, dd)
            part = pl.ds(pl.multiple_of(share * rows, rows), rows)

            def put(at, carry):
                source = array.at[base - begin + at]
                act(pltpu.make_async_copy(source, out.at[info[first + at], part], sem))
                return carry

            lax.fori_loop(begin, jnp.minimum(count, end), put, 0)
            base += end - begin


def weights_kernel(grid, table, layout, info, *refs):
    packed, (out, sem) = refs[:-2], refs[-2:]
    for act in (lambda copy: copy.start(), lambda copy: copy.wait()):
        place_blocks(grid, table, layout, 1, info, packed, out, sem, act)


def body(
    partials,
    owners,
    step_count,
    master,
    moment,
    second,
    stat_left,
    stat_right,
    basis_left,
    basis_right,
):
    grid = Grid(lax.axis_size("dp"), lax.axis_size("owner"))
    table = Table(grid, master.shape[0])
    own = partials[0]
    other = grid.swap(own, core=1)
    info, level, fetched = pl.pallas_call(
        functools.partial(table_kernel, grid, table),
        out_shape=(
            pltpu.SMEM((table.size,), jnp.int32),
            pltpu.SMEM((1,), jnp.int32),
            pltpu.VMEM(own.shape, BF16),
        ),
        in_specs=[SMEM, HBM],
        out_specs=(SMEM, SMEM, VMEM),
        scratch_shapes=[pltpu.SMEM((grid.owners,), jnp.int32), pltpu.SemaphoreType.DMA],
        compiler_params=pltpu.CompilerParams(vmem_limit_bytes=VMEM_LIMIT),
    )(
        pltpu.with_memory_space_constraint(owners, pltpu.SMEM),
        pltpu.with_memory_space_constraint(own, pltpu.HBM),
    )
    states = (master, moment, second, stat_left, stat_right, basis_left, basis_right)
    return lax.switch(
        level[0],
        [functools.partial(update, grid, table, room) for room in table.rooms],
        info,
        fetched,
        other,
        step_count,
        *states,
    )


def update(
    grid,
    table,
    room,
    info,
    own,
    other,
    step_count,
    master,
    moment,
    second,
    stat_left,
    stat_right,
    basis_left,
    basis_right,
):
    slots, size = master.shape[:2]
    blocks = own.shape[0]
    rows = size // table.shares
    chain = Chain()
    correction = 1.0 - jnp.power(jnp.float32(0.95), step_count.astype(F32))
    share = shape((table.each, rows, size), BF16)
    group_state = shape((table.each, size, size), F32)
    group_gradient = shape((table.each, size, size), BF16)
    state = shape((slots, size, size), F32)
    plane = [(dm, dd) for dm in range(grid.middle) for dd in range(grid.dp)]
    passes = slots * size**3
    relay = len(plane) == 4 and grid.dp == 2
    cuts = (0, (room + 1) // 2, room) if relay else (0, room)
    pieces = [shape((end - begin, rows, size), BF16) for begin, end in zip(cuts, cuts[1:])]

    def scatter_plane(sent):
        if not relay:
            return [sent[0][0]] + [
                grid.swap(sent[index][0], middle=dm, dp=dd) for index, (dm, dd) in enumerate(plane) if index
            ]
        mine, along_dp, along_middle, across = sent
        first_one = grid.swap(across[0], middle=1)
        first_two = grid.swap(across[1], dp=1)
        middle_one = grid.swap(along_middle[0], middle=1)
        dp_two = grid.swap(along_dp[1], dp=1)
        dp_one, middle_two = chain.call(
            merge_kernel, (), (along_dp[0], along_middle[1], first_one, first_two), pieces
        )
        dp_one, middle_two = grid.swap(dp_one, dp=1), grid.swap(middle_two, middle=1)
        return [mine[0], middle_one, dp_one, mine[1], dp_two, middle_two]

    def gather_plane(held):
        if not relay:
            got = [(grid.swap(held[0], middle=dm, dp=dd), (dm, dd), 0) for dm, dd in plane[1:]]
            return [(held[0], plane[0], 0)], got
        one, two = held
        middle_one, dp_two = grid.swap(one, middle=1), grid.swap(two, dp=1)
        middle_two, dp_one = grid.swap(two, middle=1), grid.swap(one, dp=1)
        across_one, across_two = grid.swap(middle_one, dp=1), grid.swap(dp_two, middle=1)
        early = [(one, (0, 0), 0), (two, (0, 0), 1), (middle_one, (1, 0), 0), (dp_two, (0, 1), 1)]
        late = [(middle_two, (1, 0), 1), (dp_one, (0, 1), 0), (across_one, (1, 1), 0), (across_two, (1, 1), 1)]
        return early, late

    def pack(given):
        arrays = [array for array, _, _ in given]
        entries = sum(array.shape[0] for array in arrays)
        (packed,) = chain.call(pack_kernel, (), arrays, [shape((entries, rows, size), BF16)], moved=1)
        return packed

    def over_high(arrays):
        return [arrays[0]] + [grid.swap(arrays[dh], high=dh) for dh in range(1, grid.high)]

    outs = chain.call(
        functools.partial(spread_kernel, grid, table, cuts), (info,), (own, other), pieces * len(plane)
    )
    count = len(pieces)
    got = scatter_plane([outs[index * count : (index + 1) * count] for index in range(len(plane))])
    rot_old, left_plain, left_turned, right_tall, right_turned = chain.call(
        prepare_kernel,
        (),
        (moment, basis_left, basis_right),
        [
            state,
            shape((slots, size, 2 * size), BF16),
            shape((slots, size, 2 * size), BF16),
            shape((slots, 2 * size, size), BF16),
            shape((slots, 2 * size, 2 * size), BF16),
        ],
        16 * passes,
    )
    outs = chain.call(
        functools.partial(gather_sum_kernel, grid, table, cuts),
        (info,),
        got,
        [share] * grid.high,
        scratch=(pltpu.VMEM((room, rows, size), BF16),),
    )
    (summed,) = chain.call(sum_kernel, (), over_high(outs), [share])
    parts = [summed] + [grid.swap(summed, dp=dd) for dd in range(1, table.shares)]
    gradient, turned, updated = chain.call(
        functools.partial(step_kernel, grid, table),
        (info, correction),
        (*parts, rot_old, second, master, left_plain, left_turned, right_tall, right_turned),
        [group_gradient, group_state, share],
        14 * passes,
    )
    spread = over_high([updated] * grid.high)
    others = [grid.swap(gradient, dp=dg * table.shares) for dg in range(1, table.groups)]
    bases = (stat_left, stat_right, basis_left, basis_right)
    whole = pltpu.HBM((slots, size, size), F32)
    done = chain.call(
        functools.partial(own_kernel, table),
        (info,),
        (gradient, turned, left_plain, *bases),
        [whole] * 3,
        400 * passes,
        scratch=(pltpu.VMEM((3, table.each, size, size), F32), pltpu.SemaphoreType.DMA),
        specs=[HBM] * 3,
    )
    held = chain.call(
        functools.partial(join_kernel, grid, table, cuts),
        (info,),
        (*spread, *others),
        pieces,
        scratch=(pltpu.VMEM((table.length, rows, size), BF16),),
    )
    early, late = gather_plane(held)
    layout = [[(place, cuts[piece], cuts[piece + 1]) for _, place, piece in part] for part in (early, late)]
    packed = [pack(early)]
    others_state = shape(((table.groups - 1) * table.each, size, size), F32)
    new_bases = chain.call(
        functools.partial(others_kernel, table),
        (info,),
        (*others, *bases),
        [others_state] * 2,
        400 * passes,
    )
    packed.append(pack(late))
    across = [grid.swap(array, core=1) for array in packed]
    prepared = (rot_old, second, left_plain, left_turned, right_tall, right_turned)
    weights = pltpu.HBM((blocks, size, size), BF16)
    direction, left_new, right_new, weights_own = chain.call(
        functools.partial(finish_kernel, grid, table, layout),
        (info, correction),
        (*others, *prepared, *new_bases, *packed),
        [whole] * 3 + [weights],
        100 * passes,
        scratch=(pltpu.VMEM(others_state.shape, F32), pltpu.SemaphoreType.DMA),
        specs=[HBM] * 4,
        moved=1,
        reuse=done,
    )
    (weights_all,) = chain.call(
        functools.partial(weights_kernel, grid, table, layout),
        (info,),
        across,
        [weights],
        scratch=(pltpu.SemaphoreType.DMA,),
        specs=[HBM],
        moved=1,
        reuse=(weights_own,),
    )
    return (weights_all, direction, left_new, right_new)


def solution(mesh):
    placed = (
        P(("dp", "owner"), None, None, None),
        P(),
        P(),
        P("owner", None, None),
        P("owner", None, None),
        P("owner", None, None),
        P("owner", None, None),
        P("owner", None, None),
        P("owner", None, None),
        P("owner", None, None),
    )
    return jax.shard_map(
        body,
        mesh=mesh,
        in_specs=placed,
        out_specs=(P(), P("owner", None, None), P("owner", None, None), P("owner", None, None)),
        check_vma=False,
    )
```

profile of v0, /device:TPU:0, one launch (start us, length us, event | category | flops | bytes accessed | tf_op | source)
XLA Modules:
  0.0 61.4 jit_solution(16676837609502383434)
XLA Ops:
  1.2 0.7 %copy-done = s32[48]{0:T(128)S(1)} copy-done((s32[48]{0:T(128)S(1)}, s32[48]{0:T(128)}, u32[]{:S(2)}) %copy-start) | copy-done | bytes 216
  1.8 2.0 %shard_map.129 = (s32[121]{0:T(128)S(4)}, s32[1]{0:T(128)S(4)}, bf16[48,128,128]{2,1,0:T(8,128)(2,1)S(1)}) custom-call(s32[48]{0:T(128)S(1)} %copy-done, bf16[48,128,128]{2,1,0:T(8,128)(2,1)} %bitcast.3), custom_call_target="tpu_custom_call" | custom-call | tf_op jit(solution)/shard_map/pallas_call | solution.py:433
  3.8 0.6 collective-permute-done.63
  4.4 56.8 %conditional.1 = (bf16[48,128,128]{2,1,0:T(8,128)(2,1)}, f32[6,128,128]{2,1,0:T(8,128)}, f32[6,128,128]{2,1,0:T(8,128)}, f32[6,128,128]{2,1,0:T(8,128)}) conditional(s32[]{:T(128)} %bitcast.1, (s32[1]{0:T(128)}, s32[121]{0:T(128)S(4)}, bf16[48,128,128]{2,1,0:T(8,128)(2,1)S(1)}, bf16[48,128,128]{2,1,0:T(8,128)(2,1)S(1)}, ...), branch_computations={%region_0.0_spmd, %region_1.0_spmd, %region_2.0_spmd} | conditional | flops 11702108160 | bytes 44729308 | solution.py:449
  4.4 0.6 %branch_1_fun.13 = (bf16[5,128,128]{2,1,0:T(8,128)(2,1)S(1)}, bf16[4,128,128]{2,1,0:T(8,128)(2,1)S(1)}, bf16[5,128,128]{2,1,0:T(8,128)(2,1)S(1)}, bf16[4,128,128...) custom-call(s32[121]{0:T(128)S(4)} %get-tuple-element.126.refs_0_, ...), custom_call_target="tpu_custom_call" | custom-call | bytes 4325376 | tf_op jit(solution)/shard_map/cond/branch_1_fun/pallas_call | solution.py:43
  5.1 2.9 %collective-permute-start.22 = (bf16[5,128,128]{2,1,0:T(8,128)(2,1)S(1)}, bf16[5,128,128]{2,1,0:T(8,128)(2,1)S(1)}, u32[]{:S(2)}, u32[]{:S(2)}) collective-permute-start(bf16[5,128,128]{2,1,0:T(8,128)(2,1)S(1)} %get-tuple-element.134), channel_id=1, source_target_pairs={{0,2},{1,3},{2,0},{3,1},{4,6},{5,7},{6,4},{7,5},{8,10},{9,11},{10,... | collective-permute-start | bytes 491528 | tf_op jit(solution)/shard_map/cond/branch_1_fun/ppermute | solution.py:78
  8.0 1.5 %collective-permute-start.23 = (bf16[4,128,128]{2,1,0:T(8,128)(2,1)S(1)}, bf16[4,128,128]{2,1,0:T(8,128)(2,1)S(1)}, u32[]{:S(2)}, u32[]{:S(2)}) collective-permute-start(bf16[4,128,128]{2,1,0:T(8,128)(2,1)S(1)} %get-tuple-element.135), channel_id=1, source_target_pairs={{0,16},{1,17},{2,18},{3,19},{4,20},{5,21},{6,22},{7,23},{8,24},{9,... | collective-permute-start | bytes 393224 | tf_op jit(solution)/shard_map/cond/branch_1_fun/ppermute | solution.py:78
  10.1 3.2 %collective-permute-done.23.refs_3_ = bf16[4,128,128]{2,1,0:T(8,128)(2,1)S(1)} collective-permute-done((bf16[4,128,128]{2,1,0:T(8,128)(2,1)S(1)}, bf16[4,128,128]{2,1,0:T(8,128)(2,1)S(1)}, u32[]{:S(2)}, u32[]{:S(2)}) %collective-permute-start.23) | collective-permute-done | bytes 131104 | tf_op jit(solution)/shard_map/cond/branch_1_fun/ppermute | solution.py:78
  13.4 1.9 %collective-permute-start.24 = (bf16[5,128,128]{2,1,0:T(8,128)(2,1)S(1)}, bf16[5,128,128]{2,1,0:T(8,128)(2,1)S(1)}, u32[]{:S(2)}, u32[]{:S(2)}) collective-permute-start(bf16[5,128,128]{2,1,0:T(8,128)(2,1)S(1)} %get-tuple-element.137), channel_id=1, source_target_pairs={{0,16},{1,17},{2,18},{3,19},{4,20},{5,21},{6,22},{7,23},{8,24},{9,... | collective-permute-start | bytes 491528 | tf_op jit(solution)/shard_map/cond/branch_1_fun/ppermute | solution.py:78
  15.5 1.8 %collective-permute-start.26 = (bf16[4,128,128]{2,1,0:T(8,128)(2,1)S(1)}, bf16[4,128,128]{2,1,0:T(8,128)(2,1)S(1)}, u32[]{:S(2)}, u32[]{:S(2)}) collective-permute-start(bf16[4,128,128]{2,1,0:T(8,128)(2,1)S(1)} %get-tuple-element.140), channel_id=1, source_target_pairs={{0,2},{1,3},{2,0},{3,1},{4,6},{5,7},{6,4},{7,5},{8,10},{9,11},{10,... | collective-permute-start | bytes 393224 | tf_op jit(solution)/shard_map/cond/branch_1_fun/ppermute | solution.py:78
  17.2 0.6 branch_1_fun.15
  17.8 3.6 %collective-permute-done.25.refs_5_ = bf16[4,128,128]{2,1,0:T(8,128)(2,1)S(1)} collective-permute-done((bf16[4,128,128]{2,1,0:T(8,128)(2,1)S(1)}, bf16[4,128,128]{2,1,0:T(8,128)(2,1)S(1)}, u32[]{:S(2)}, u32[]{:S(2)}) %collective-permute-start.25) | collective-permute-done | bytes 131104 | tf_op jit(solution)/shard_map/cond/branch_1_fun/ppermute | solution.py:78
  21.5 1.6 %collective-permute-start.27 = (bf16[3,128,128]{2,1,0:T(8,128)(2,1)S(1)}, bf16[3,128,128]{2,1,0:T(8,128)(2,1)S(1)}, u32[]{:S(2)}, u32[]{:S(2)}) collective-permute-start(bf16[3,128,128]{2,1,0:T(8,128)(2,1)S(1)} %get-tuple-element.147), channel_id=1, source_target_pairs={{0,4},{1,5},{2,6},{3,7},{4,0},{5,1},{6,2},{7,3},{8,12},{9,13},{10,... | collective-permute-start | bytes 294920 | tf_op jit(solution)/shard_map/cond/branch_1_fun/ppermute | solution.py:78
  23.2 2.6 %collective-permute-start.28 = (bf16[3,128,128]{2,1,0:T(8,128)(2,1)S(1)}, bf16[3,128,128]{2,1,0:T(8,128)(2,1)S(1)}, u32[]{:S(2)}, u32[]{:S(2)}) collective-permute-start(bf16[3,128,128]{2,1,0:T(8,128)(2,1)S(1)} %get-tuple-element.148), channel_id=1, source_target_pairs={{0,8},{1,9},{2,10},{3,11},{4,12},{5,13},{6,14},{7,15},{8,0},{9,1},... | collective-permute-start | bytes 294920 | tf_op jit(solution)/shard_map/cond/branch_1_fun/ppermute | solution.py:78
  26.7 4.0 %collective-permute-done.28.refs_2_ = bf16[3,128,128]{2,1,0:T(8,128)(2,1)S(1)} collective-permute-done((bf16[3,128,128]{2,1,0:T(8,128)(2,1)S(1)}, bf16[3,128,128]{2,1,0:T(8,128)(2,1)S(1)}, u32[]{:S(2)}, u32[]{:S(2)}) %collective-permute-start.28) | collective-permute-done | bytes 98336 | tf_op jit(solution)/shard_map/cond/branch_1_fun/ppermute | solution.py:78
  30.7 1.6 %collective-permute-done.29.refs_3_ = bf16[3,128,128]{2,1,0:T(8,128)(2,1)S(1)} collective-permute-done((bf16[3,128,128]{2,1,0:T(8,128)(2,1)S(1)}, bf16[3,128,128]{2,1,0:T(8,128)(2,1)S(1)}, u32[]{:S(2)}, u32[]{:S(2)}) %collective-permute-start.29) | collective-permute-done | bytes 98336 | tf_op jit(solution)/shard_map/cond/branch_1_fun/ppermute | solution.py:78
  32.4 0.8 %branch_1_fun.18 = (bf16[3,128,128]{2,1,0:T(8,128)(2,1)S(1)}, f32[3,128,128]{2,1,0:T(8,128)S(1)}, bf16[3,128,128]{2,1,0:T(8,128)(2,1)S(1)}, f32[8,128]{1,0:T(8,128)S(1)}) custom-call(s32[121]{0:T(128)S(4)} %get-tuple-element.126.refs_0_, f32[1]{0:T(128)S(6)} %sub.7.refs_1_, bf16[3,128,128]{2,1,0:T(8,128)(2,1)S(1)} %get-tuple-element.151.refs_2_, ...), custom_call_target="tpu_custom_call" | custom-call | flops 176160768 | bytes 3637248 | tf_op jit(solution)/shard_map/cond/branch_1_fun/pallas_call | solution.py:43
  33.2 1.8 %collective-permute-start.32 = (bf16[3,128,128]{2,1,0:T(8,128)(2,1)S(1)}, bf16[3,128,128]{2,1,0:T(8,128)(2,1)S(1)}, u32[]{:S(2)}, u32[]{:S(2)}) collective-permute-start(bf16[3,128,128]{2,1,0:T(8,128)(2,1)S(1)} %get-tuple-element.160.refs_1_), channel_id=1, source_target_pairs={{0,12},{1,13},{2,14},{3,15},{4,8},{5,9},{6,10},{7,11},{8,4},{9,5},... | collective-permute-start | bytes 294920 | tf_op jit(solution)/shard_map/cond/branch_1_fun/ppermute | solution.py:78
  35.1 1.2 %collective-permute-start.31 = (bf16[3,128,128]{2,1,0:T(8,128)(2,1)S(1)}, bf16[3,128,128]{2,1,0:T(8,128)(2,1)S(1)}, u32[]{:S(2)}, u32[]{:S(2)}) collective-permute-start(bf16[3,128,128]{2,1,0:T(8,128)(2,1)S(1)} %get-tuple-element.160.refs_1_), channel_id=1, source_target_pairs={{0,8},{1,9},{2,10},{3,11},{4,12},{5,13},{6,14},{7,15},{8,0},{9,1},... | collective-permute-start | bytes 294920 | tf_op jit(solution)/shard_map/cond/branch_1_fun/ppermute | solution.py:78
  36.3 1.4 %collective-permute-start.30 = (bf16[3,128,128]{2,1,0:T(8,128)(2,1)S(1)}, bf16[3,128,128]{2,1,0:T(8,128)(2,1)S(1)}, u32[]{:S(2)}, u32[]{:S(2)}) collective-permute-start(bf16[3,128,128]{2,1,0:T(8,128)(2,1)S(1)} %get-tuple-element.160.refs_1_), channel_id=1, source_target_pairs={{0,4},{1,5},{2,6},{3,7},{4,0},{5,1},{6,2},{7,3},{8,12},{9,13},{10,... | collective-permute-start | bytes 294920 | tf_op jit(solution)/shard_map/cond/branch_1_fun/ppermute | solution.py:78
  37.7 1.5 %collective-permute-start.33 = (bf16[3,128,128]{2,1,0:T(8,128)(2,1)S(1)}, bf16[3,128,128]{2,1,0:T(8,128)(2,1)S(1)}, u32[]{:S(2)}, u32[]{:S(2)}) collective-permute-start(bf16[3,128,128]{2,1,0:T(8,128)(2,1)S(1)} %get-tuple-element.161.refs_1_), channel_id=1, source_target_pairs={{0,16},{1,17},{2,18},{3,19},{4,20},{5,21},{6,22},{7,23},{8,24},{9,... | collective-permute-start | bytes 294920 | tf_op jit(solution)/shard_map/cond/branch_1_fun/ppermute | solution.py:78
  39.2 4.0 %branch_1_fun.19 = (f32[6,128,128]{2,1,0:T(8,128)}, f32[6,128,128]{2,1,0:T(8,128)}, f32[6,128,128]{2,1,0:T(8,128)}, f32[8,128]{1,0:T(8,128)S(1)}) custom-call(s32[121]{0:T(128)S(4)} %get-tuple-element.126.refs_0_, bf16[3,128,128]{2,1,0:T(8,128)(2,1)S(1)} %get-tuple-element.161.refs_1_, f32[3,128,128]{2,1,0:T(8,128)S(1)} %get-tuple-element.162.refs_2_, ...), custom_call_target="tpu_custom_call" | custom-call | flops 5033164800 | bytes 3440640 | tf_op jit(solution)/shard_map/cond/branch_1_fun/pallas_call | solution.py:43
  43.3 1.4 %collective-permute-start.34 = (bf16[5,128,128]{2,1,0:T(8,128)(2,1)S(1)}, bf16[5,128,128]{2,1,0:T(8,128)(2,1)S(1)}, u32[]{:S(2)}, u32[]{:S(2)}) collective-permute-start(bf16[5,128,128]{2,1,0:T(8,128)(2,1)S(1)} %get-tuple-element.167.refs_0_), channel_id=1, source_target_pairs={{0,2},{1,3},{2,0},{3,1},{4,6},{5,7},{6,4},{7,5},{8,10},{9,11},{10,... | collective-permute-start | bytes 491528 | tf_op jit(solution)/shard_map/cond/branch_1_fun/ppermute | solution.py:78
  44.7 1.4 %collective-permute-start.35 = (bf16[4,128,128]{2,1,0:T(8,128)(2,1)S(1)}, bf16[4,128,128]{2,1,0:T(8,128)(2,1)S(1)}, u32[]{:S(2)}, u32[]{:S(2)}) collective-permute-start(bf16[4,128,128]{2,1,0:T(8,128)(2,1)S(1)} %get-tuple-element.168.refs_1_), channel_id=1, source_target_pairs={{0,16},{1,17},{2,18},{3,19},{4,20},{5,21},{6,22},{7,23},{8,24},{9,... | collective-permute-start | bytes 393224 | tf_op jit(solution)/shard_map/cond/branch_1_fun/ppermute | solution.py:78
  46.5 1.0 %collective-permute-start.38 = (bf16[5,128,128]{2,1,0:T(8,128)(2,1)S(1)}, bf16[5,128,128]{2,1,0:T(8,128)(2,1)S(1)}, u32[]{:S(2)}, u32[]{:S(2)}) collective-permute-start(bf16[5,128,128]{2,1,0:T(8,128)(2,1)S(1)} %get-tuple-element.167.refs_0_), channel_id=1, source_target_pairs={{0,16},{1,17},{2,18},{3,19},{4,20},{5,21},{6,22},{7,23},{8,24},{9,... | collective-permute-start | bytes 491528 | tf_op jit(solution)/shard_map/cond/branch_1_fun/ppermute | solution.py:78
  47.5 2.2 %collective-permute-done.35.refs_3_ = bf16[4,128,128]{2,1,0:T(8,128)(2,1)S(1)} collective-permute-done((bf16[4,128,128]{2,1,0:T(8,128)(2,1)S(1)}, bf16[4,128,128]{2,1,0:T(8,128)(2,1)S(1)}, u32[]{:S(2)}, u32[]{:S(2)}) %collective-permute-start.35) | collective-permute-done | bytes 131104 | tf_op jit(solution)/shard_map/cond/branch_1_fun/ppermute | solution.py:78
  49.7 0.7 %collective-permute-start.40 = (bf16[4,128,128]{2,1,0:T(8,128)(2,1)S(1)}, bf16[4,128,128]{2,1,0:T(8,128)(2,1)S(1)}, u32[]{:S(2)}, u32[]{:S(2)}) collective-permute-start(bf16[4,128,128]{2,1,0:T(8,128)(2,1)S(1)} %collective-permute-done.35.refs_3_), channel_id=1, source_target_pairs={{0,2},{1,3},{2,0},{3,1},{4,6},{5,7},{6,4},{7,5},{8,10},{9,11},{10,... | collective-permute-start | bytes 393224 | tf_op jit(solution)/shard_map/cond/branch_1_fun/ppermute | solution.py:78
  50.5 1.1 %collective-permute-start.39 = (bf16[5,128,128]{2,1,0:T(8,128)(2,1)S(1)}, bf16[5,128,128]{2,1,0:T(8,128)(2,1)S(1)}, u32[]{:S(2)}, u32[]{:S(2)}) collective-permute-start(bf16[5,128,128]{2,1,0:T(8,128)(2,1)S(1)} %collective-permute-done.34.refs_2_), channel_id=1, source_target_pairs={{0,16},{1,17},{2,18},{3,19},{4,20},{5,21},{6,22},{7,23},{8,24},{9,... | collective-permute-start | bytes 491528 | tf_op jit(solution)/shard_map/cond/branch_1_fun/ppermute | solution.py:78
  51.6 3.2 %branch_1_fun.22 = (f32[3,128,128]{2,1,0:T(8,128)S(1)}, f32[3,128,128]{2,1,0:T(8,128)S(1)}, f32[8,128]{1,0:T(8,128)S(1)}) custom-call(s32[121]{0:T(128)S(4)} %get-tuple-element.126.refs_0_, bf16[3,128,128]{2,1,0:T(8,128)(2,1)S(1)} %collective-permute-done.33.refs_5_.refs_1_.refs_2_, f32[6,128,128]{2,1,0:T(8,128)S(1)} %copy-done.9, ...), custom_call_target="tpu_custom_call" | custom-call | flops 5033164800 | bytes 2064384 | tf_op jit(solution)/shard_map/cond/branch_1_fun/pallas_call | solution.py:43
  54.9 2.3 %collective-permute-done.39.refs_2_ = bf16[5,128,128]{2,1,0:T(8,128)(2,1)S(1)} collective-permute-done((bf16[5,128,128]{2,1,0:T(8,128)(2,1)S(1)}, bf16[5,128,128]{2,1,0:T(8,128)(2,1)S(1)}, u32[]{:S(2)}, u32[]{:S(2)}) %collective-permute-start.39) | collective-permute-done | bytes 163872 | tf_op jit(solution)/shard_map/cond/branch_1_fun/ppermute | solution.py:78
  57.3 1.8 %branch_1_fun.24 = (f32[6,128,128]{2,1,0:T(8,128)}, f32[6,128,128]{2,1,0:T(8,128)}, f32[6,128,128]{2,1,0:T(8,128)}, bf16[48,128,128]{2,1,0:T(8,128)(2,1)}, f32[8,128]{1,0:T(8,128)S(1)}) custom-call(s32[121]{0:T(128)S(4)} %get-tuple-element.126.refs_0_, f32[1]{0:T(128)S(6)} %sub.7.refs_1_, ...), custom_call_target="tpu_custom_call", output_to_operand_aliasing={{0}: (14, {}), {1}: (15, {}), {2}: (16, {})} | custom-call | flops 1258291200 | bytes 1 | tf_op jit(solution)/shard_map/cond/branch_1_fun/pallas_call | solution.py:43
  59.2 1.5 %branch_1_fun.25 = (bf16[48,128,128]{2,1,0:T(8,128)(2,1)}, f32[8,128]{1,0:T(8,128)}) custom-call(s32[121]{0:T(128)S(4)} %get-tuple-element.126.refs_0_, bf16[18,128,128]{2,1,0:T(8,128)(2,1)S(1)} %collective-permute-done.36.refs_1_, bf16[18,128,128]{2,1,0:T(8,128)(2,1)S(1)} %collective-permute-done.41.refs_2_, ...), custom_call_target="tpu_custom_call", output_to_operand_aliasing={{0}: (4, {})} | custom-call | bytes 1 | tf_op jit(solution)/shard_map/cond/branch_1_fun/pallas_call | solution.py:43
  (43 shorter events, 2.7 us)
Async XLA Ops:
  0.6 3.8 %collective-permute-start.63 = (bf16[48,128,128]{2,1,0:T(8,128)(2,1)}, bf16[48,128,128]{2,1,0:T(8,128)(2,1)S(1)}, u32[]{:S(2)}, u32[]{:S(2)}) collective-permute-start(bf16[48,128,128]{2,1,0:T(8,128)(2,1)} %bitcast.2), channel_id=1, source_target_pairs={{0,1},{1,0},{2,3},{3,2},{4,5},{5,4},{6,7},{7,6},{8,9},{9,8},{10,11... | collective-permute-start | bytes 4718600 | tf_op jit(solution)/shard_map/ppermute | solution.py:78
  1.2 0.7 %copy-start = (s32[48]{0:T(128)S(1)}, s32[48]{0:T(128)}, u32[]{:S(2)}) copy-start(s32[48]{0:T(128)} %owners.1) | copy-start | bytes 580
  1.8 2.6 %copy-start.1 = (f32[6,128,128]{2,1,0:T(8,128)S(1)}, f32[6,128,128]{2,1,0:T(8,128)}, u32[]{:S(2)}) copy-start(f32[6,128,128]{2,1,0:T(8,128)} %param.18) | copy-start | bytes 1179652
  1.8 2.6 %copy-start.2 = (f32[6,128,128]{2,1,0:T(8,128)S(1)}, f32[6,128,128]{2,1,0:T(8,128)}, u32[]{:S(2)}) copy-start(f32[6,128,128]{2,1,0:T(8,128)} %param.16) | copy-start | bytes 1179652
  1.8 2.6 %copy-start.3 = (f32[6,128,128]{2,1,0:T(8,128)S(1)}, f32[6,128,128]{2,1,0:T(8,128)}, u32[]{:S(2)}) copy-start(f32[6,128,128]{2,1,0:T(8,128)} %param.17) | copy-start | bytes 1179652
  1.8 2.6 %copy-start.4 = (f32[6,128,128]{2,1,0:T(8,128)S(1)}, f32[6,128,128]{2,1,0:T(8,128)}, u32[]{:S(2)}) copy-start(f32[6,128,128]{2,1,0:T(8,128)} %param.21) | copy-start | bytes 1179652
  4.4 12.8 %copy-start.6 = (f32[6,128,128]{2,1,0:T(8,128)S(1)}, f32[6,128,128]{2,1,0:T(8,128)}, u32[]{:S(2)}) copy-start(f32[6,128,128]{2,1,0:T(8,128)} %get-tuple-element.143.refs_2_.refs_7_.refs_5_) | copy-start | bytes 1179652 | tf_op jit(solution)/shard_map/cond
  5.1 8.2 %collective-permute-start.22 = (bf16[5,128,128]{2,1,0:T(8,128)(2,1)S(1)}, bf16[5,128,128]{2,1,0:T(8,128)(2,1)S(1)}, u32[]{:S(2)}, u32[]{:S(2)}) collective-permute-start(bf16[5,128,128]{2,1,0:T(8,128)(2,1)S(1)} %get-tuple-element.134), channel_id=1, source_target_pairs={{0,2},{1,3},{2,0},{3,1},{4,6},{5,7},{6,4},{7,5},{8,10},{9,11},{10,... | collective-permute-start | bytes 491528 | tf_op jit(solution)/shard_map/cond/branch_1_fun/ppermute | solution.py:78
  8.0 5.3 %collective-permute-start.23 = (bf16[4,128,128]{2,1,0:T(8,128)(2,1)S(1)}, bf16[4,128,128]{2,1,0:T(8,128)(2,1)S(1)}, u32[]{:S(2)}, u32[]{:S(2)}) collective-permute-start(bf16[4,128,128]{2,1,0:T(8,128)(2,1)S(1)} %get-tuple-element.135), channel_id=1, source_target_pairs={{0,16},{1,17},{2,18},{3,19},{4,20},{5,21},{6,22},{7,23},{8,24},{9,... | collective-permute-start | bytes 393224 | tf_op jit(solution)/shard_map/cond/branch_1_fun/ppermute | solution.py:78
  9.6 11.8 %collective-permute-start.21 = (bf16[5,128,128]{2,1,0:T(8,128)(2,1)S(1)}, bf16[5,128,128]{2,1,0:T(8,128)(2,1)S(1)}, u32[]{:S(2)}, u32[]{:S(2)}) collective-permute-start(bf16[5,128,128]{2,1,0:T(8,128)(2,1)S(1)} %get-tuple-element.131), channel_id=1, source_target_pairs={{0,2},{1,3},{2,0},{3,1},{4,6},{5,7},{6,4},{7,5},{8,10},{9,11},{10,... | collective-permute-start | bytes 491528 | tf_op jit(solution)/shard_map/cond/branch_1_fun/ppermute | solution.py:78
  13.4 8.0 %collective-permute-start.24 = (bf16[5,128,128]{2,1,0:T(8,128)(2,1)S(1)}, bf16[5,128,128]{2,1,0:T(8,128)(2,1)S(1)}, u32[]{:S(2)}, u32[]{:S(2)}) collective-permute-start(bf16[5,128,128]{2,1,0:T(8,128)(2,1)S(1)} %get-tuple-element.137), channel_id=1, source_target_pairs={{0,16},{1,17},{2,18},{3,19},{4,20},{5,21},{6,22},{7,23},{8,24},{9,... | collective-permute-start | bytes 491528 | tf_op jit(solution)/shard_map/cond/branch_1_fun/ppermute | solution.py:78
  15.2 6.1 %collective-permute-start.25 = (bf16[4,128,128]{2,1,0:T(8,128)(2,1)S(1)}, bf16[4,128,128]{2,1,0:T(8,128)(2,1)S(1)}, u32[]{:S(2)}, u32[]{:S(2)}) collective-permute-start(bf16[4,128,128]{2,1,0:T(8,128)(2,1)S(1)} %get-tuple-element.139), channel_id=1, source_target_pairs={{0,16},{1,17},{2,18},{3,19},{4,20},{5,21},{6,22},{7,23},{8,24},{9,... | collective-permute-start | bytes 393224 | tf_op jit(solution)/shard_map/cond/branch_1_fun/ppermute | solution.py:78
  15.5 5.9 %collective-permute-start.26 = (bf16[4,128,128]{2,1,0:T(8,128)(2,1)S(1)}, bf16[4,128,128]{2,1,0:T(8,128)(2,1)S(1)}, u32[]{:S(2)}, u32[]{:S(2)}) collective-permute-start(bf16[4,128,128]{2,1,0:T(8,128)(2,1)S(1)} %get-tuple-element.140), channel_id=1, source_target_pairs={{0,2},{1,3},{2,0},{3,1},{4,6},{5,7},{6,4},{7,5},{8,10},{9,11},{10,... | collective-permute-start | bytes 393224 | tf_op jit(solution)/shard_map/cond/branch_1_fun/ppermute | solution.py:78
  21.5 5.1 %collective-permute-start.27 = (bf16[3,128,128]{2,1,0:T(8,128)(2,1)S(1)}, bf16[3,128,128]{2,1,0:T(8,128)(2,1)S(1)}, u32[]{:S(2)}, u32[]{:S(2)}) collective-permute-start(bf16[3,128,128]{2,1,0:T(8,128)(2,1)S(1)} %get-tuple-element.147), channel_id=1, source_target_pairs={{0,4},{1,5},{2,6},{3,7},{4,0},{5,1},{6,2},{7,3},{8,12},{9,13},{10,... | collective-permute-start | bytes 294920 | tf_op jit(solution)/shard_map/cond/branch_1_fun/ppermute | solution.py:78
  23.2 7.5 %collective-permute-start.28 = (bf16[3,128,128]{2,1,0:T(8,128)(2,1)S(1)}, bf16[3,128,128]{2,1,0:T(8,128)(2,1)S(1)}, u32[]{:S(2)}, u32[]{:S(2)}) collective-permute-start(bf16[3,128,128]{2,1,0:T(8,128)(2,1)S(1)} %get-tuple-element.148), channel_id=1, source_target_pairs={{0,8},{1,9},{2,10},{3,11},{4,12},{5,13},{6,14},{7,15},{8,0},{9,1},... | collective-permute-start | bytes 294920 | tf_op jit(solution)/shard_map/cond/branch_1_fun/ppermute | solution.py:78
  25.8 6.5 %collective-permute-start.29 = (bf16[3,128,128]{2,1,0:T(8,128)(2,1)S(1)}, bf16[3,128,128]{2,1,0:T(8,128)(2,1)S(1)}, u32[]{:S(2)}, u32[]{:S(2)}) collective-permute-start(bf16[3,128,128]{2,1,0:T(8,128)(2,1)S(1)} %get-tuple-element.149), channel_id=1, source_target_pairs={{0,12},{1,13},{2,14},{3,15},{4,8},{5,9},{6,10},{7,11},{8,4},{9,5},... | collective-permute-start | bytes 294920 | tf_op jit(solution)/shard_map/cond/branch_1_fun/ppermute | solution.py:78
  32.4 6.8 %copy-start.9 = (f32[6,128,128]{2,1,0:T(8,128)S(1)}, f32[6,128,128]{2,1,0:T(8,128)}, u32[]{:S(2)}) copy-start(f32[6,128,128]{2,1,0:T(8,128)} %get-tuple-element.163.refs_4_.refs_2_) | copy-start | bytes 1179652 | tf_op jit(solution)/shard_map/cond
  32.4 6.8 %copy-start.12 = (f32[6,128,128]{2,1,0:T(8,128)S(1)}, f32[6,128,128]{2,1,0:T(8,128)}, u32[]{:S(2)}) copy-start(f32[6,128,128]{2,1,0:T(8,128)} %get-tuple-element.164.refs_5_.refs_3_) | copy-start | bytes 1179652 | tf_op jit(solution)/shard_map/cond
  33.2 10.0 %collective-permute-start.32 = (bf16[3,128,128]{2,1,0:T(8,128)(2,1)S(1)}, bf16[3,128,128]{2,1,0:T(8,128)(2,1)S(1)}, u32[]{:S(2)}, u32[]{:S(2)}) collective-permute-start(bf16[3,128,128]{2,1,0:T(8,128)(2,1)S(1)} %get-tuple-element.160.refs_1_), channel_id=1, source_target_pairs={{0,12},{1,13},{2,14},{3,15},{4,8},{5,9},{6,10},{7,11},{8,4},{9,5},... | collective-permute-start | bytes 294920 | tf_op jit(solution)/shard_map/cond/branch_1_fun/ppermute | solution.py:78
  35.1 8.2 %collective-permute-start.31 = (bf16[3,128,128]{2,1,0:T(8,128)(2,1)S(1)}, bf16[3,128,128]{2,1,0:T(8,128)(2,1)S(1)}, u32[]{:S(2)}, u32[]{:S(2)}) collective-permute-start(bf16[3,128,128]{2,1,0:T(8,128)(2,1)S(1)} %get-tuple-element.160.refs_1_), channel_id=1, source_target_pairs={{0,8},{1,9},{2,10},{3,11},{4,12},{5,13},{6,14},{7,15},{8,0},{9,1},... | collective-permute-start | bytes 294920 | tf_op jit(solution)/shard_map/cond/branch_1_fun/ppermute | solution.py:78
  36.3 7.0 %collective-permute-start.30 = (bf16[3,128,128]{2,1,0:T(8,128)(2,1)S(1)}, bf16[3,128,128]{2,1,0:T(8,128)(2,1)S(1)}, u32[]{:S(2)}, u32[]{:S(2)}) collective-permute-start(bf16[3,128,128]{2,1,0:T(8,128)(2,1)S(1)} %get-tuple-element.160.refs_1_), channel_id=1, source_target_pairs={{0,4},{1,5},{2,6},{3,7},{4,0},{5,1},{6,2},{7,3},{8,12},{9,13},{10,... | collective-permute-start | bytes 294920 | tf_op jit(solution)/shard_map/cond/branch_1_fun/ppermute | solution.py:78
  37.7 5.6 %collective-permute-start.33 = (bf16[3,128,128]{2,1,0:T(8,128)(2,1)S(1)}, bf16[3,128,128]{2,1,0:T(8,128)(2,1)S(1)}, u32[]{:S(2)}, u32[]{:S(2)}) collective-permute-start(bf16[3,128,128]{2,1,0:T(8,128)(2,1)S(1)} %get-tuple-element.161.refs_1_), channel_id=1, source_target_pairs={{0,16},{1,17},{2,18},{3,19},{4,20},{5,21},{6,22},{7,23},{8,24},{9,... | collective-permute-start | bytes 294920 | tf_op jit(solution)/shard_map/cond/branch_1_fun/ppermute | solution.py:78
  43.3 7.1 %collective-permute-start.34 = (bf16[5,128,128]{2,1,0:T(8,128)(2,1)S(1)}, bf16[5,128,128]{2,1,0:T(8,128)(2,1)S(1)}, u32[]{:S(2)}, u32[]{:S(2)}) collective-permute-start(bf16[5,128,128]{2,1,0:T(8,128)(2,1)S(1)} %get-tuple-element.167.refs_0_), channel_id=1, source_target_pairs={{0,2},{1,3},{2,0},{3,1},{4,6},{5,7},{6,4},{7,5},{8,10},{9,11},{10,... | collective-permute-start | bytes 491528 | tf_op jit(solution)/shard_map/cond/branch_1_fun/ppermute | solution.py:78
  44.7 5.0 %collective-permute-start.35 = (bf16[4,128,128]{2,1,0:T(8,128)(2,1)S(1)}, bf16[4,128,128]{2,1,0:T(8,128)(2,1)S(1)}, u32[]{:S(2)}, u32[]{:S(2)}) collective-permute-start(bf16[4,128,128]{2,1,0:T(8,128)(2,1)S(1)} %get-tuple-element.168.refs_1_), channel_id=1, source_target_pairs={{0,16},{1,17},{2,18},{3,19},{4,20},{5,21},{6,22},{7,23},{8,24},{9,... | collective-permute-start | bytes 393224 | tf_op jit(solution)/shard_map/cond/branch_1_fun/ppermute | solution.py:78
  46.1 8.8 %collective-permute-start.37 = (bf16[4,128,128]{2,1,0:T(8,128)(2,1)S(1)}, bf16[4,128,128]{2,1,0:T(8,128)(2,1)S(1)}, u32[]{:S(2)}, u32[]{:S(2)}) collective-permute-start(bf16[4,128,128]{2,1,0:T(8,128)(2,1)S(1)} %get-tuple-element.168.refs_1_), channel_id=1, source_target_pairs={{0,2},{1,3},{2,0},{3,1},{4,6},{5,7},{6,4},{7,5},{8,10},{9,11},{10,... | collective-permute-start | bytes 393224 | tf_op jit(solution)/shard_map/cond/branch_1_fun/ppermute | solution.py:78
  46.5 8.4 %collective-permute-start.38 = (bf16[5,128,128]{2,1,0:T(8,128)(2,1)S(1)}, bf16[5,128,128]{2,1,0:T(8,128)(2,1)S(1)}, u32[]{:S(2)}, u32[]{:S(2)}) collective-permute-start(bf16[5,128,128]{2,1,0:T(8,128)(2,1)S(1)} %get-tuple-element.167.refs_0_), channel_id=1, source_target_pairs={{0,16},{1,17},{2,18},{3,19},{4,20},{5,21},{6,22},{7,23},{8,24},{9,... | collective-permute-start | bytes 491528 | tf_op jit(solution)/shard_map/cond/branch_1_fun/ppermute | solution.py:78
  49.7 5.2 %collective-permute-start.40 = (bf16[4,128,128]{2,1,0:T(8,128)(2,1)S(1)}, bf16[4,128,128]{2,1,0:T(8,128)(2,1)S(1)}, u32[]{:S(2)}, u32[]{:S(2)}) collective-permute-start(bf16[4,128,128]{2,1,0:T(8,128)(2,1)S(1)} %collective-permute-done.35.refs_3_), channel_id=1, source_target_pairs={{0,2},{1,3},{2,0},{3,1},{4,6},{5,7},{6,4},{7,5},{8,10},{9,11},{10,... | collective-permute-start | bytes 393224 | tf_op jit(solution)/shard_map/cond/branch_1_fun/ppermute | solution.py:78
  50.4 8.6 %collective-permute-start.36 = (bf16[18,128,128]{2,1,0:T(8,128)(2,1)S(1)}, bf16[18,128,128]{2,1,0:T(8,128)(2,1)S(1)}, u32[]{:S(2)}, u32[]{:S(2)}) collective-permute-start(bf16[18,128,128]{2,1,0:T(8,128)(2,1)S(1)} %get-tuple-element.170.refs_11_), channel_id=1, source_target_pairs={{0,1},{1,0},{2,3},{3,2},{4,5},{5,4},{6,7},{7,6},{8,9},{9,8},{10,11... | collective-permute-start | bytes 1769480 | tf_op jit(solution)/shard_map/cond/branch_1_fun/ppermute | solution.py:78
  50.5 6.6 %collective-permute-start.39 = (bf16[5,128,128]{2,1,0:T(8,128)(2,1)S(1)}, bf16[5,128,128]{2,1,0:T(8,128)(2,1)S(1)}, u32[]{:S(2)}, u32[]{:S(2)}) collective-permute-start(bf16[5,128,128]{2,1,0:T(8,128)(2,1)S(1)} %collective-permute-done.34.refs_2_), channel_id=1, source_target_pairs={{0,16},{1,17},{2,18},{3,19},{4,20},{5,21},{6,22},{7,23},{8,24},{9,... | collective-permute-start | bytes 491528 | tf_op jit(solution)/shard_map/cond/branch_1_fun/ppermute | solution.py:78
  57.2 2.1 %collective-permute-start.41 = (bf16[18,128,128]{2,1,0:T(8,128)(2,1)S(1)}, bf16[18,128,128]{2,1,0:T(8,128)(2,1)S(1)}, u32[]{:S(2)}, u32[]{:S(2)}) collective-permute-start(bf16[18,128,128]{2,1,0:T(8,128)(2,1)S(1)} %get-tuple-element.173.refs_12_), channel_id=1, source_target_pairs={{0,1},{1,0},{2,3},{3,2},{4,5},{5,4},{6,7},{7,6},{8,9},{9,8},{10,11... | collective-permute-start | bytes 1769480 | tf_op jit(solution)/shard_map/cond/branch_1_fun/ppermute | solution.py:78
where the time goes:
time: 61.4 us
  starting transfers between devices  25.9 us (42%)
  waiting for transfers between devices  17.7 us (29%)
  Pallas kernels  14.8 us (24%)
  loops' own time  1.39 us (2%)
  between operations  0.84 us (1%)
  local copies, waits for them, and re-layouts  0.69 us (1%)
    ppermute x22, starting transfers between devices, swap(): return lax.ppermute(array, AXES, pairs)  25.9 us
    ppermute x22, waiting for transfers between devices, swap(): return lax.ppermute(array, AXES, pairs)  17.7 us
    pallas_call x13, Pallas kernels, call(): pl.pallas_call(run, out_shape=(*outs, shape((8, 128), F32)), in_specs=[SM...  12.9 us
    pallas_call x1, Pallas kernels, body(): pl.pallas_call(functools.partial(table_kernel, grid, table), out_shape=(p...  1.96 us
    another operation x1, loops' own time, body(): lax.switch(level[0], [functools.partial(update, grid, table, room) for ro...  1.39 us
  transfers between devices with their start and end apart: 22, of which 8 were waited for; matrix products, arithmetic and copies ran while one was open for 0% of the time, Pallas kernels for 19%

commit v1 on v0

--- a/solution.py
+++ b/solution.py
@@ -333,9 +333,14 @@
     count = table.groups - 1
     gradients, refs = refs[:count], refs[count:]
     (rot_old, second, left_plain, left_turned, right_tall, right_turned) = refs[:6]
-    new_left, new_right, *packed = refs[6 : 8 + len(layout)]
-    direction, left_out, right_out, weights, held, sem = refs[8 + len(layout) :]
-    place_blocks(grid, table, layout, 0, info, packed, weights, sem, lambda copy: copy.start())
+    new_left, new_right, across, *packed = refs[6 : 9 + len(layout)]
+    direction, left_out, right_out, weights, held, sem = refs[9 + len(layout) :]
+
+    def place(act):
+        place_blocks(grid, table, layout[:1], 1, info, [across], weights, sem, act)
+        place_blocks(grid, table, layout, 0, info, packed, weights, sem, act)
+
+    place(lambda copy: copy.start())
     group = lax.div(info[table.place], table.shares)
     every = [
         (dg, index, table.slot(info, group ^ dg, index))
@@ -361,12 +366,13 @@
             copies[-1].start()
     for copy in copies:
         copy.wait()
-    place_blocks(grid, table, layout, 0, info, packed, weights, sem, lambda copy: copy.wait())
+    place(lambda copy: copy.wait())
 
 
 def join_kernel(grid, table, cuts, info, *refs):
     pieces = len(cuts) - 1
-    arrays, outs, every = refs[: grid.high], refs[-1 - pieces : -1], refs[-1]
+    outs, every = refs[-1 - pieces : -1], refs[-1]
+    arrays = dict(zip((1, 2, 3, 0), refs))
     spare = info[table.counts + part_index(grid, table, info)]
     for dh in range(grid.high):
         first = table.inverse + (info[table.place + 1] ^ dh) * table.each
@@ -550,7 +556,7 @@
         [share] * grid.high,
         scratch=(pltpu.VMEM((room, rows, size), BF16),),
     )
-    (summed,) = chain.call(sum_kernel, (), over_high(outs), [share])
+    (summed,) = chain.call(sum_kernel, (), [over_high(outs)[dh] for dh in (3, 2, 1, 0)], [share])
     parts = [summed] + [grid.swap(summed, dp=dd) for dd in range(1, table.shares)]
     gradient, turned, updated = chain.call(
         functools.partial(step_kernel, grid, table),
@@ -575,7 +581,7 @@
     held = chain.call(
         functools.partial(join_kernel, grid, table, cuts),
         (info,),
-        (*spread, *others),
+        (*(spread[dh] for dh in (1, 2, 3, 0)), *others),
         pieces,
         scratch=(pltpu.VMEM((table.length, rows, size), BF16),),
     )
@@ -597,7 +603,7 @@
     direction, left_new, right_new, weights_own = chain.call(
         functools.partial(finish_kernel, grid, table, layout),
         (info, correction),
-        (*others, *prepared, *new_bases, *packed),
+        (*others, *prepared, *new_bases, across[0], *packed),
         [whole] * 3 + [weights],
         100 * passes,
         scratch=(pltpu.VMEM(others_state.shape, F32), pltpu.SemaphoreType.DMA),
@@ -606,9 +612,9 @@
         reuse=done,
     )
     (weights_all,) = chain.call(
-        functools.partial(weights_kernel, grid, table, layout),
+        functools.partial(weights_kernel, grid, table, layout[1:]),
         (info,),
-        across,
+        across[1:],
         [weights],
         scratch=(pltpu.SemaphoreType.DMA,),
         specs=[HBM],

time: 61.4 us -> 57.1 us (0.930)
  starting transfers between devices: 25.9 us -> 22.5 us
    ppermute x22, starting transfers between devices: 25.9 us -> 22.5 us  [swap(): return lax.ppermute(array, AXES, pairs)]
  transfers between devices with their start and end apart: 22 -> 22, of which waited for: 8 -> 14; matrix products, arithmetic and copies ran while one was open for 0% -> 0% of each run, Pallas kernels for 19% -> 21%
where the time goes in v1:
time: 57.1 us
  starting transfers between devices  22.5 us (39%)
  waiting for transfers between devices  17.4 us (30%)
  Pallas kernels  14.7 us (26%)
  loops' own time  1.12 us (2%)
  between operations  0.84 us (1%)
  local copies, waits for them, and re-layouts  0.69 us (1%)
    ppermute x22, starting transfers between devices, swap(): return lax.ppermute(array, AXES, pairs)  22.5 us
    ppermute x22, waiting for transfers between devices, swap(): return lax.ppermute(array, AXES, pairs)  17.4 us
    pallas_call x13, Pallas kernels, call(): pl.pallas_call(run, out_shape=(*outs, shape((8, 128), F32)), in_specs=[SM...  12.7 us
    pallas_call x1, Pallas kernels, body(): pl.pallas_call(functools.partial(table_kernel, grid, table), out_shape=(p...  1.96 us
  transfers between devices with their start and end apart: 22, of which 14 were waited for; matrix products, arithmetic and copies ran while one was open for 0% of the time, Pallas kernels for 21%

profile of v1, /device:TPU:0, one launch (start us, length us, event | category | flops | bytes accessed | tf_op | source)
XLA Modules:
  0.0 57.1 jit_solution(15641673068088240257)
XLA Ops:
  1.2 0.7 %copy-done = s32[48]{0:T(128)S(1)} copy-done((s32[48]{0:T(128)S(1)}, s32[48]{0:T(128)}, u32[]{:S(2)}) %copy-start) | copy-done | bytes 216
  1.8 2.0 %shard_map.129 = (s32[121]{0:T(128)S(4)}, s32[1]{0:T(128)S(4)}, bf16[48,128,128]{2,1,0:T(8,128)(2,1)S(1)}) custom-call(s32[48]{0:T(128)S(1)} %copy-done, bf16[48,128,128]{2,1,0:T(8,128)(2,1)} %bitcast.3), custom_call_target="tpu_custom_call" | custom-call | tf_op jit(solution)/shard_map/pallas_call | solution.py:439
  3.8 0.6 %collective-permute-done.63 = bf16[48,128,128]{2,1,0:T(8,128)(2,1)S(1)} collective-permute-done((bf16[48,128,128]{2,1,0:T(8,128)(2,1)}, bf16[48,128,128]{2,1,0:T(8,128)(2,1)S(1)}, u32[]{:S(2)}, u32[]{:S(2)}) %collective-permute-start.63) | collective-permute-done | bytes 1572896 | tf_op jit(solution)/shard_map/ppermute | solution.py:78
  4.4 52.6 %conditional.1 = (bf16[48,128,128]{2,1,0:T(8,128)(2,1)}, f32[6,128,128]{2,1,0:T(8,128)}, f32[6,128,128]{2,1,0:T(8,128)}, f32[6,128,128]{2,1,0:T(8,128)}) conditional(s32[]{:T(128)} %bitcast.1, (s32[1]{0:T(128)}, s32[121]{0:T(128)S(4)}, bf16[48,128,128]{2,1,0:T(8,128)(2,1)S(1)}, bf16[48,128,128]{2,1,0:T(8,128)(2,1)S(1)}, ...), branch_computations={%region_0.0_spmd, %region_1.0_spmd, %region_2.0_spmd} | conditional | flops 11702108160 | bytes 44729308 | solution.py:455
  4.9 2.9 %collective-permute-start.1 = (bf16[4,128,128]{2,1,0:T(8,128)(2,1)S(1)}, bf16[4,128,128]{2,1,0:T(8,128)(2,1)S(1)}, u32[]{:S(2)}, u32[]{:S(2)}) collective-permute-start(bf16[4,128,128]{2,1,0:T(8,128)(2,1)S(1)} %get-tuple-element.74), channel_id=1, source_target_pairs={{0,2},{1,3},{2,0},{3,1},{4,6},{5,7},{6,4},{7,5},{8,10},{9,11},{10,... | collective-permute-start | bytes 393224 | tf_op jit(solution)/shard_map/cond/branch_0_fun/ppermute | solution.py:78
  7.8 1.5 %collective-permute-start.2 = (bf16[4,128,128]{2,1,0:T(8,128)(2,1)S(1)}, bf16[4,128,128]{2,1,0:T(8,128)(2,1)S(1)}, u32[]{:S(2)}, u32[]{:S(2)}) collective-permute-start(bf16[4,128,128]{2,1,0:T(8,128)(2,1)S(1)} %get-tuple-element.75), channel_id=1, source_target_pairs={{0,16},{1,17},{2,18},{3,19},{4,20},{5,21},{6,22},{7,23},{8,24},{9,... | collective-permute-start | bytes 393224 | tf_op jit(solution)/shard_map/cond/branch_0_fun/ppermute | solution.py:78
  9.9 1.8 %collective-permute-done.1.refs_2_ = bf16[4,128,128]{2,1,0:T(8,128)(2,1)S(1)} collective-permute-done((bf16[4,128,128]{2,1,0:T(8,128)(2,1)S(1)}, bf16[4,128,128]{2,1,0:T(8,128)(2,1)S(1)}, u32[]{:S(2)}, u32[]{:S(2)}) %collective-permute-start.1) | collective-permute-done | bytes 131104 | tf_op jit(solution)/shard_map/cond/branch_0_fun/ppermute | solution.py:78
  11.7 2.5 %collective-permute-done.2.refs_3_ = bf16[4,128,128]{2,1,0:T(8,128)(2,1)S(1)} collective-permute-done((bf16[4,128,128]{2,1,0:T(8,128)(2,1)S(1)}, bf16[4,128,128]{2,1,0:T(8,128)(2,1)S(1)}, u32[]{:S(2)}, u32[]{:S(2)}) %collective-permute-start.2) | collective-permute-done | bytes 131104 | tf_op jit(solution)/shard_map/cond/branch_0_fun/ppermute | solution.py:78
  14.3 1.6 %collective-permute-start.3 = (bf16[4,128,128]{2,1,0:T(8,128)(2,1)S(1)}, bf16[4,128,128]{2,1,0:T(8,128)(2,1)S(1)}, u32[]{:S(2)}, u32[]{:S(2)}) collective-permute-start(bf16[4,128,128]{2,1,0:T(8,128)(2,1)S(1)} %get-tuple-element.77), channel_id=1, source_target_pairs={{0,16},{1,17},{2,18},{3,19},{4,20},{5,21},{6,22},{7,23},{8,24},{9,... | collective-permute-start | bytes 393224 | tf_op jit(solution)/shard_map/cond/branch_0_fun/ppermute | solution.py:78
  16.4 0.5 branch_0_fun.15
  17.0 2.3 %collective-permute-done.3.refs_3_ = bf16[4,128,128]{2,1,0:T(8,128)(2,1)S(1)} collective-permute-done((bf16[4,128,128]{2,1,0:T(8,128)(2,1)S(1)}, bf16[4,128,128]{2,1,0:T(8,128)(2,1)S(1)}, u32[]{:S(2)}, u32[]{:S(2)}) %collective-permute-start.3) | collective-permute-done | bytes 131104 | tf_op jit(solution)/shard_map/cond/branch_0_fun/ppermute | solution.py:78
  19.3 1.5 %collective-permute-done.5.refs_6_ = bf16[4,128,128]{2,1,0:T(8,128)(2,1)S(1)} collective-permute-done((bf16[4,128,128]{2,1,0:T(8,128)(2,1)S(1)}, bf16[4,128,128]{2,1,0:T(8,128)(2,1)S(1)}, u32[]{:S(2)}, u32[]{:S(2)}) %collective-permute-start.5) | collective-permute-done | bytes 131104 | tf_op jit(solution)/shard_map/cond/branch_0_fun/ppermute | solution.py:78
  21.0 3.7 %collective-permute-start.6 = (bf16[3,128,128]{2,1,0:T(8,128)(2,1)S(1)}, bf16[3,128,128]{2,1,0:T(8,128)(2,1)S(1)}, u32[]{:S(2)}, u32[]{:S(2)}) collective-permute-start(bf16[3,128,128]{2,1,0:T(8,128)(2,1)S(1)} %get-tuple-element.86), channel_id=1, source_target_pairs={{0,12},{1,13},{2,14},{3,15},{4,8},{5,9},{6,10},{7,11},{8,4},{9,5},... | collective-permute-start | bytes 294920 | tf_op jit(solution)/shard_map/cond/branch_0_fun/ppermute | solution.py:78
  24.6 0.8 %collective-permute-start.8 = (bf16[3,128,128]{2,1,0:T(8,128)(2,1)S(1)}, bf16[3,128,128]{2,1,0:T(8,128)(2,1)S(1)}, u32[]{:S(2)}, u32[]{:S(2)}) collective-permute-start(bf16[3,128,128]{2,1,0:T(8,128)(2,1)S(1)} %get-tuple-element.88), channel_id=1, source_target_pairs={{0,4},{1,5},{2,6},{3,7},{4,0},{5,1},{6,2},{7,3},{8,12},{9,13},{10,... | collective-permute-start | bytes 294920 | tf_op jit(solution)/shard_map/cond/branch_0_fun/ppermute | solution.py:78
  26.1 1.5 %collective-permute-done.6.refs_0_ = bf16[3,128,128]{2,1,0:T(8,128)(2,1)S(1)} collective-permute-done((bf16[3,128,128]{2,1,0:T(8,128)(2,1)S(1)}, bf16[3,128,128]{2,1,0:T(8,128)(2,1)S(1)}, u32[]{:S(2)}, u32[]{:S(2)}) %collective-permute-start.6) | collective-permute-done | bytes 98336 | tf_op jit(solution)/shard_map/cond/branch_0_fun/ppermute | solution.py:78
  27.6 3.2 %collective-permute-done.7.refs_1_ = bf16[3,128,128]{2,1,0:T(8,128)(2,1)S(1)} collective-permute-done((bf16[3,128,128]{2,1,0:T(8,128)(2,1)S(1)}, bf16[3,128,128]{2,1,0:T(8,128)(2,1)S(1)}, u32[]{:S(2)}, u32[]{:S(2)}) %collective-permute-start.7) | collective-permute-done | bytes 98336 | tf_op jit(solution)/shard_map/cond/branch_0_fun/ppermute | solution.py:78
  31.0 0.8 %branch_0_fun.18 = (bf16[3,128,128]{2,1,0:T(8,128)(2,1)S(1)}, f32[3,128,128]{2,1,0:T(8,128)S(1)}, bf16[3,128,128]{2,1,0:T(8,128)(2,1)S(1)}, f32[8,128]{1,0:T(8,128)S(1)}) custom-call(s32[121]{0:T(128)S(4)} %get-tuple-element.66.refs_0_, f32[1]{0:T(128)S(6)} %sub.6.refs_1_, bf16[3,128,128]{2,1,0:T(8,128)(2,1)S(1)} %get-tuple-element.91.refs_2_, ...), custom_call_target="tpu_custom_call" | custom-call | flops 176160768 | bytes 3637248 | tf_op jit(solution)/shard_map/cond/branch_0_fun/pallas_call | solution.py:43
  31.8 2.1 %collective-permute-start.10 = (bf16[3,128,128]{2,1,0:T(8,128)(2,1)S(1)}, bf16[3,128,128]{2,1,0:T(8,128)(2,1)S(1)}, u32[]{:S(2)}, u32[]{:S(2)}) collective-permute-start(bf16[3,128,128]{2,1,0:T(8,128)(2,1)S(1)} %get-tuple-element.100.refs_4_), channel_id=1, source_target_pairs={{0,8},{1,9},{2,10},{3,11},{4,12},{5,13},{6,14},{7,15},{8,0},{9,1},... | collective-permute-start | bytes 294920 | tf_op jit(solution)/shard_map/cond/branch_0_fun/ppermute | solution.py:78
  34.0 1.7 %collective-permute-start.11 = (bf16[3,128,128]{2,1,0:T(8,128)(2,1)S(1)}, bf16[3,128,128]{2,1,0:T(8,128)(2,1)S(1)}, u32[]{:S(2)}, u32[]{:S(2)}) collective-permute-start(bf16[3,128,128]{2,1,0:T(8,128)(2,1)S(1)} %get-tuple-element.100.refs_4_), channel_id=1, source_target_pairs={{0,12},{1,13},{2,14},{3,15},{4,8},{5,9},{6,10},{7,11},{8,4},{9,5},... | collective-permute-start | bytes 294920 | tf_op jit(solution)/shard_map/cond/branch_0_fun/ppermute | solution.py:78
  35.7 4.0 %branch_0_fun.19 = (f32[6,128,128]{2,1,0:T(8,128)}, f32[6,128,128]{2,1,0:T(8,128)}, f32[6,128,128]{2,1,0:T(8,128)}, f32[8,128]{1,0:T(8,128)S(1)}) custom-call(s32[121]{0:T(128)S(4)} %get-tuple-element.66.refs_0_, bf16[3,128,128]{2,1,0:T(8,128)(2,1)S(1)} %get-tuple-element.101.refs_1_, f32[3,128,128]{2,1,0:T(8,128)S(1)} %get-tuple-element.102.refs_2_, ...), custom_call_target="tpu_custom_call" | custom-call | flops 5033164800 | bytes 3440640 | tf_op jit(solution)/shard_map/cond/branch_0_fun/pallas_call | solution.py:43
  39.7 0.8 %collective-permute-done.11.refs_3_ = bf16[3,128,128]{2,1,0:T(8,128)(2,1)S(1)} collective-permute-done((bf16[3,128,128]{2,1,0:T(8,128)(2,1)S(1)}, bf16[3,128,128]{2,1,0:T(8,128)(2,1)S(1)}, u32[]{:S(2)}, u32[]{:S(2)}) %collective-permute-start.11) | collective-permute-done | bytes 98336 | tf_op jit(solution)/shard_map/cond/branch_0_fun/ppermute | solution.py:78
  40.5 0.8 %collective-permute-done.9.refs_1_ = bf16[3,128,128]{2,1,0:T(8,128)(2,1)S(1)} collective-permute-done((bf16[3,128,128]{2,1,0:T(8,128)(2,1)S(1)}, bf16[3,128,128]{2,1,0:T(8,128)(2,1)S(1)}, u32[]{:S(2)}, u32[]{:S(2)}) %collective-permute-start.9) | collective-permute-done | bytes 98336 | tf_op jit(solution)/shard_map/cond/branch_0_fun/ppermute | solution.py:78
  41.7 0.9 %collective-permute-start.17 = (bf16[4,128,128]{2,1,0:T(8,128)(2,1)S(1)}, bf16[4,128,128]{2,1,0:T(8,128)(2,1)S(1)}, u32[]{:S(2)}, u32[]{:S(2)}) collective-permute-start(bf16[4,128,128]{2,1,0:T(8,128)(2,1)S(1)} %get-tuple-element.107.refs_1_), channel_id=1, source_target_pairs={{0,16},{1,17},{2,18},{3,19},{4,20},{5,21},{6,22},{7,23},{8,24},{9,... | collective-permute-start | bytes 393224 | tf_op jit(solution)/shard_map/cond/branch_0_fun/ppermute | solution.py:78
  42.6 1.3 %collective-permute-start.13 = (bf16[4,128,128]{2,1,0:T(8,128)(2,1)S(1)}, bf16[4,128,128]{2,1,0:T(8,128)(2,1)S(1)}, u32[]{:S(2)}, u32[]{:S(2)}) collective-permute-start(bf16[4,128,128]{2,1,0:T(8,128)(2,1)S(1)} %get-tuple-element.107.refs_1_), channel_id=1, source_target_pairs={{0,2},{1,3},{2,0},{3,1},{4,6},{5,7},{6,4},{7,5},{8,10},{9,11},{10,... | collective-permute-start | bytes 393224 | tf_op jit(solution)/shard_map/cond/branch_0_fun/ppermute | solution.py:78
  43.9 1.6 %collective-permute-start.14 = (bf16[4,128,128]{2,1,0:T(8,128)(2,1)S(1)}, bf16[4,128,128]{2,1,0:T(8,128)(2,1)S(1)}, u32[]{:S(2)}, u32[]{:S(2)}) collective-permute-start(bf16[4,128,128]{2,1,0:T(8,128)(2,1)S(1)} %get-tuple-element.108.refs_0_), channel_id=1, source_target_pairs={{0,16},{1,17},{2,18},{3,19},{4,20},{5,21},{6,22},{7,23},{8,24},{9,... | collective-permute-start | bytes 393224 | tf_op jit(solution)/shard_map/cond/branch_0_fun/ppermute | solution.py:78
  45.5 0.9 %collective-permute-done.15.refs_2_ = bf16[4,128,128]{2,1,0:T(8,128)(2,1)S(1)} collective-permute-done((bf16[4,128,128]{2,1,0:T(8,128)(2,1)S(1)}, bf16[4,128,128]{2,1,0:T(8,128)(2,1)S(1)}, u32[]{:S(2)}, u32[]{:S(2)}) %collective-permute-start.15) | collective-permute-done | bytes 131104 | tf_op jit(solution)/shard_map/cond/branch_0_fun/ppermute | solution.py:78
  46.8 0.9 %collective-permute-start.16 = (bf16[4,128,128]{2,1,0:T(8,128)(2,1)S(1)}, bf16[4,128,128]{2,1,0:T(8,128)(2,1)S(1)}, u32[]{:S(2)}, u32[]{:S(2)}) collective-permute-start(bf16[4,128,128]{2,1,0:T(8,128)(2,1)S(1)} %collective-permute-done.15.refs_2_), channel_id=1, source_target_pairs={{0,16},{1,17},{2,18},{3,19},{4,20},{5,21},{6,22},{7,23},{8,24},{9,... | collective-permute-start | bytes 393224 | tf_op jit(solution)/shard_map/cond/branch_0_fun/ppermute | solution.py:78
  47.7 1.3 %collective-permute-start.18 = (bf16[4,128,128]{2,1,0:T(8,128)(2,1)S(1)}, bf16[4,128,128]{2,1,0:T(8,128)(2,1)S(1)}, u32[]{:S(2)}, u32[]{:S(2)}) collective-permute-start(bf16[4,128,128]{2,1,0:T(8,128)(2,1)S(1)} %collective-permute-done.17.refs_3_), channel_id=1, source_target_pairs={{0,2},{1,3},{2,0},{3,1},{4,6},{5,7},{6,4},{7,5},{8,10},{9,11},{10,... | collective-permute-start | bytes 393224 | tf_op jit(solution)/shard_map/cond/branch_0_fun/ppermute | solution.py:78
  49.1 3.2 %branch_0_fun.22 = (f32[3,128,128]{2,1,0:T(8,128)S(1)}, f32[3,128,128]{2,1,0:T(8,128)S(1)}, f32[8,128]{1,0:T(8,128)S(1)}) custom-call(s32[121]{0:T(128)S(4)} %get-tuple-element.66.refs_0_, bf16[3,128,128]{2,1,0:T(8,128)(2,1)S(1)} %collective-permute-done.12.refs_5_.refs_1_.refs_2_, f32[6,128,128]{2,1,0:T(8,128)S(1)} %copy-done.8, ...), custom_call_target="tpu_custom_call" | custom-call | flops 5033164800 | bytes 2064384 | tf_op jit(solution)/shard_map/cond/branch_0_fun/pallas_call | solution.py:43
  52.7 0.6 %collective-permute-done.18.refs_3_ = bf16[4,128,128]{2,1,0:T(8,128)(2,1)S(1)} collective-permute-done((bf16[4,128,128]{2,1,0:T(8,128)(2,1)S(1)}, bf16[4,128,128]{2,1,0:T(8,128)(2,1)S(1)}, u32[]{:S(2)}, u32[]{:S(2)}) %collective-permute-start.18) | collective-permute-done | bytes 131104 | tf_op jit(solution)/shard_map/cond/branch_0_fun/ppermute | solution.py:78
  53.4 2.0 %branch_0_fun.24 = (f32[6,128,128]{2,1,0:T(8,128)}, f32[6,128,128]{2,1,0:T(8,128)}, f32[6,128,128]{2,1,0:T(8,128)}, bf16[48,128,128]{2,1,0:T(8,128)(2,1)}, f32[8,128]{1,0:T(8,128)S(1)}) custom-call(s32[121]{0:T(128)S(4)} %get-tuple-element.66.refs_0_, f32[1]{0:T(128)S(6)} %sub.6.refs_1_, ...), custom_call_target="tpu_custom_call", output_to_operand_aliasing={{0}: (15, {}), {1}: (16, {}), {2}: (17, {})} | custom-call | flops 1258291200 | bytes 1 | tf_op jit(solution)/shard_map/cond/branch_0_fun/pallas_call | solution.py:43
  55.4 1.3 %branch_0_fun.25 = (bf16[48,128,128]{2,1,0:T(8,128)(2,1)}, f32[8,128]{1,0:T(8,128)}) custom-call(s32[121]{0:T(128)S(4)} %get-tuple-element.66.refs_0_, bf16[16,128,128]{2,1,0:T(8,128)(2,1)S(1)} %collective-permute-done.19.refs_1_, f32[8,128]{1,0:T(8,128)S(1)} %get-tuple-element.120.refs_2_, ...), custom_call_target="tpu_custom_call", output_to_operand_aliasing={{0}: (3, {})} | custom-call | bytes 1 | tf_op jit(solution)/shard_map/cond/branch_0_fun/pallas_call | solution.py:43
  (43 shorter events, 3.7 us)
Async XLA Ops:
  0.6 3.8 %collective-permute-start.63 = (bf16[48,128,128]{2,1,0:T(8,128)(2,1)}, bf16[48,128,128]{2,1,0:T(8,128)(2,1)S(1)}, u32[]{:S(2)}, u32[]{:S(2)}) collective-permute-start(bf16[48,128,128]{2,1,0:T(8,128)(2,1)} %bitcast.2), channel_id=1, source_target_pairs={{0,1},{1,0},{2,3},{3,2},{4,5},{5,4},{6,7},{7,6},{8,9},{9,8},{10,11... | collective-permute-start | bytes 4718600 | tf_op jit(solution)/shard_map/ppermute | solution.py:78
  1.2 0.7 %copy-start = (s32[48]{0:T(128)S(1)}, s32[48]{0:T(128)}, u32[]{:S(2)}) copy-start(s32[48]{0:T(128)} %owners.1) | copy-start | bytes 580
  1.8 2.6 %copy-start.1 = (f32[6,128,128]{2,1,0:T(8,128)S(1)}, f32[6,128,128]{2,1,0:T(8,128)}, u32[]{:S(2)}) copy-start(f32[6,128,128]{2,1,0:T(8,128)} %param.18) | copy-start | bytes 1179652
  1.8 2.6 %copy-start.2 = (f32[6,128,128]{2,1,0:T(8,128)S(1)}, f32[6,128,128]{2,1,0:T(8,128)}, u32[]{:S(2)}) copy-start(f32[6,128,128]{2,1,0:T(8,128)} %param.16) | copy-start | bytes 1179652
  1.8 2.6 %copy-start.3 = (f32[6,128,128]{2,1,0:T(8,128)S(1)}, f32[6,128,128]{2,1,0:T(8,128)}, u32[]{:S(2)}) copy-start(f32[6,128,128]{2,1,0:T(8,128)} %param.17) | copy-start | bytes 1179652
  1.8 2.6 %copy-start.4 = (f32[6,128,128]{2,1,0:T(8,128)S(1)}, f32[6,128,128]{2,1,0:T(8,128)}, u32[]{:S(2)}) copy-start(f32[6,128,128]{2,1,0:T(8,128)} %param.21) | copy-start | bytes 1179652
  4.4 12.0 %copy-start.5 = (f32[6,128,128]{2,1,0:T(8,128)S(1)}, f32[6,128,128]{2,1,0:T(8,128)}, u32[]{:S(2)}) copy-start(f32[6,128,128]{2,1,0:T(8,128)} %get-tuple-element.83.refs_2_.refs_7_.refs_5_) | copy-start | bytes 1179652 | tf_op jit(solution)/shard_map/cond
  4.9 6.8 %collective-permute-start.1 = (bf16[4,128,128]{2,1,0:T(8,128)(2,1)S(1)}, bf16[4,128,128]{2,1,0:T(8,128)(2,1)S(1)}, u32[]{:S(2)}, u32[]{:S(2)}) collective-permute-start(bf16[4,128,128]{2,1,0:T(8,128)(2,1)S(1)} %get-tuple-element.74), channel_id=1, source_target_pairs={{0,2},{1,3},{2,0},{3,1},{4,6},{5,7},{6,4},{7,5},{8,10},{9,11},{10,... | collective-permute-start | bytes 393224 | tf_op jit(solution)/shard_map/cond/branch_0_fun/ppermute | solution.py:78
  7.8 6.4 %collective-permute-start.2 = (bf16[4,128,128]{2,1,0:T(8,128)(2,1)S(1)}, bf16[4,128,128]{2,1,0:T(8,128)(2,1)S(1)}, u32[]{:S(2)}, u32[]{:S(2)}) collective-permute-start(bf16[4,128,128]{2,1,0:T(8,128)(2,1)S(1)} %get-tuple-element.75), channel_id=1, source_target_pairs={{0,16},{1,17},{2,18},{3,19},{4,20},{5,21},{6,22},{7,23},{8,24},{9,... | collective-permute-start | bytes 393224 | tf_op jit(solution)/shard_map/cond/branch_0_fun/ppermute | solution.py:78
  9.3 7.6 %collective-permute-start = (bf16[4,128,128]{2,1,0:T(8,128)(2,1)S(1)}, bf16[4,128,128]{2,1,0:T(8,128)(2,1)S(1)}, u32[]{:S(2)}, u32[]{:S(2)}) collective-permute-start(bf16[4,128,128]{2,1,0:T(8,128)(2,1)S(1)} %get-tuple-element.71), channel_id=1, source_target_pairs={{0,2},{1,3},{2,0},{3,1},{4,6},{5,7},{6,4},{7,5},{8,10},{9,11},{10,... | collective-permute-start | bytes 393224 | tf_op jit(solution)/shard_map/cond/branch_0_fun/ppermute | solution.py:78
  9.9 7.1 %collective-permute-start.4 = (bf16[4,128,128]{2,1,0:T(8,128)(2,1)S(1)}, bf16[4,128,128]{2,1,0:T(8,128)(2,1)S(1)}, u32[]{:S(2)}, u32[]{:S(2)}) collective-permute-start(bf16[4,128,128]{2,1,0:T(8,128)(2,1)S(1)} %get-tuple-element.79), channel_id=1, source_target_pairs={{0,16},{1,17},{2,18},{3,19},{4,20},{5,21},{6,22},{7,23},{8,24},{9,... | collective-permute-start | bytes 393224 | tf_op jit(solution)/shard_map/cond/branch_0_fun/ppermute | solution.py:78
  14.3 5.0 %collective-permute-start.3 = (bf16[4,128,128]{2,1,0:T(8,128)(2,1)S(1)}, bf16[4,128,128]{2,1,0:T(8,128)(2,1)S(1)}, u32[]{:S(2)}, u32[]{:S(2)}) collective-permute-start(bf16[4,128,128]{2,1,0:T(8,128)(2,1)S(1)} %get-tuple-element.77), channel_id=1, source_target_pairs={{0,16},{1,17},{2,18},{3,19},{4,20},{5,21},{6,22},{7,23},{8,24},{9,... | collective-permute-start | bytes 393224 | tf_op jit(solution)/shard_map/cond/branch_0_fun/ppermute | solution.py:78
  15.9 5.0 %collective-permute-start.5 = (bf16[4,128,128]{2,1,0:T(8,128)(2,1)S(1)}, bf16[4,128,128]{2,1,0:T(8,128)(2,1)S(1)}, u32[]{:S(2)}, u32[]{:S(2)}) collective-permute-start(bf16[4,128,128]{2,1,0:T(8,128)(2,1)S(1)} %get-tuple-element.80), channel_id=1, source_target_pairs={{0,2},{1,3},{2,0},{3,1},{4,6},{5,7},{6,4},{7,5},{8,10},{9,11},{10,... | collective-permute-start | bytes 393224 | tf_op jit(solution)/shard_map/cond/branch_0_fun/ppermute | solution.py:78
  21.0 6.6 %collective-permute-start.6 = (bf16[3,128,128]{2,1,0:T(8,128)(2,1)S(1)}, bf16[3,128,128]{2,1,0:T(8,128)(2,1)S(1)}, u32[]{:S(2)}, u32[]{:S(2)}) collective-permute-start(bf16[3,128,128]{2,1,0:T(8,128)(2,1)S(1)} %get-tuple-element.86), channel_id=1, source_target_pairs={{0,12},{1,13},{2,14},{3,15},{4,8},{5,9},{6,10},{7,11},{8,4},{9,5},... | collective-permute-start | bytes 294920 | tf_op jit(solution)/shard_map/cond/branch_0_fun/ppermute | solution.py:78
  24.6 6.2 %collective-permute-start.7 = (bf16[3,128,128]{2,1,0:T(8,128)(2,1)S(1)}, bf16[3,128,128]{2,1,0:T(8,128)(2,1)S(1)}, u32[]{:S(2)}, u32[]{:S(2)}) collective-permute-start(bf16[3,128,128]{2,1,0:T(8,128)(2,1)S(1)} %get-tuple-element.87), channel_id=1, source_target_pairs={{0,8},{1,9},{2,10},{3,11},{4,12},{5,13},{6,14},{7,15},{8,0},{9,1},... | collective-permute-start | bytes 294920 | tf_op jit(solution)/shard_map/cond/branch_0_fun/ppermute | solution.py:78
  24.6 6.3 %collective-permute-start.8 = (bf16[3,128,128]{2,1,0:T(8,128)(2,1)S(1)}, bf16[3,128,128]{2,1,0:T(8,128)(2,1)S(1)}, u32[]{:S(2)}, u32[]{:S(2)}) collective-permute-start(bf16[3,128,128]{2,1,0:T(8,128)(2,1)S(1)} %get-tuple-element.88), channel_id=1, source_target_pairs={{0,4},{1,5},{2,6},{3,7},{4,0},{5,1},{6,2},{7,3},{8,12},{9,13},{10,... | collective-permute-start | bytes 294920 | tf_op jit(solution)/shard_map/cond/branch_0_fun/ppermute | solution.py:78
  31.0 4.7 %copy-start.8 = (f32[6,128,128]{2,1,0:T(8,128)S(1)}, f32[6,128,128]{2,1,0:T(8,128)}, u32[]{:S(2)}) copy-start(f32[6,128,128]{2,1,0:T(8,128)} %get-tuple-element.103.refs_4_.refs_2_) | copy-start | bytes 1179652 | tf_op jit(solution)/shard_map/cond
  31.0 4.7 %copy-start.11 = (f32[6,128,128]{2,1,0:T(8,128)S(1)}, f32[6,128,128]{2,1,0:T(8,128)}, u32[]{:S(2)}) copy-start(f32[6,128,128]{2,1,0:T(8,128)} %get-tuple-element.104.refs_5_.refs_3_) | copy-start | bytes 1179652 | tf_op jit(solution)/shard_map/cond
  31.8 7.9 %collective-permute-start.10 = (bf16[3,128,128]{2,1,0:T(8,128)(2,1)S(1)}, bf16[3,128,128]{2,1,0:T(8,128)(2,1)S(1)}, u32[]{:S(2)}, u32[]{:S(2)}) collective-permute-start(bf16[3,128,128]{2,1,0:T(8,128)(2,1)S(1)} %get-tuple-element.100.refs_4_), channel_id=1, source_target_pairs={{0,8},{1,9},{2,10},{3,11},{4,12},{5,13},{6,14},{7,15},{8,0},{9,1},... | collective-permute-start | bytes 294920 | tf_op jit(solution)/shard_map/cond/branch_0_fun/ppermute | solution.py:78
  34.0 6.6 %collective-permute-start.11 = (bf16[3,128,128]{2,1,0:T(8,128)(2,1)S(1)}, bf16[3,128,128]{2,1,0:T(8,128)(2,1)S(1)}, u32[]{:S(2)}, u32[]{:S(2)}) collective-permute-start(bf16[3,128,128]{2,1,0:T(8,128)(2,1)S(1)} %get-tuple-element.100.refs_4_), channel_id=1, source_target_pairs={{0,12},{1,13},{2,14},{3,15},{4,8},{5,9},{6,10},{7,11},{8,4},{9,5},... | collective-permute-start | bytes 294920 | tf_op jit(solution)/shard_map/cond/branch_0_fun/ppermute | solution.py:78
  35.6 5.7 %collective-permute-start.9 = (bf16[3,128,128]{2,1,0:T(8,128)(2,1)S(1)}, bf16[3,128,128]{2,1,0:T(8,128)(2,1)S(1)}, u32[]{:S(2)}, u32[]{:S(2)}) collective-permute-start(bf16[3,128,128]{2,1,0:T(8,128)(2,1)S(1)} %get-tuple-element.100.refs_4_), channel_id=1, source_target_pairs={{0,4},{1,5},{2,6},{3,7},{4,0},{5,1},{6,2},{7,3},{8,12},{9,13},{10,... | collective-permute-start | bytes 294920 | tf_op jit(solution)/shard_map/cond/branch_0_fun/ppermute | solution.py:78
  35.7 4.9 %collective-permute-start.12 = (bf16[3,128,128]{2,1,0:T(8,128)(2,1)S(1)}, bf16[3,128,128]{2,1,0:T(8,128)(2,1)S(1)}, u32[]{:S(2)}, u32[]{:S(2)}) collective-permute-start(bf16[3,128,128]{2,1,0:T(8,128)(2,1)S(1)} %get-tuple-element.101.refs_1_), channel_id=1, source_target_pairs={{0,16},{1,17},{2,18},{3,19},{4,20},{5,21},{6,22},{7,23},{8,24},{9,... | collective-permute-start | bytes 294920 | tf_op jit(solution)/shard_map/cond/branch_0_fun/ppermute | solution.py:78
  41.4 5.0 %collective-permute-start.15 = (bf16[4,128,128]{2,1,0:T(8,128)(2,1)S(1)}, bf16[4,128,128]{2,1,0:T(8,128)(2,1)S(1)}, u32[]{:S(2)}, u32[]{:S(2)}) collective-permute-start(bf16[4,128,128]{2,1,0:T(8,128)(2,1)S(1)} %get-tuple-element.108.refs_0_), channel_id=1, source_target_pairs={{0,2},{1,3},{2,0},{3,1},{4,6},{5,7},{6,4},{7,5},{8,10},{9,11},{10,... | collective-permute-start | bytes 393224 | tf_op jit(solution)/shard_map/cond/branch_0_fun/ppermute | solution.py:78
  41.7 5.0 %collective-permute-start.17 = (bf16[4,128,128]{2,1,0:T(8,128)(2,1)S(1)}, bf16[4,128,128]{2,1,0:T(8,128)(2,1)S(1)}, u32[]{:S(2)}, u32[]{:S(2)}) collective-permute-start(bf16[4,128,128]{2,1,0:T(8,128)(2,1)S(1)} %get-tuple-element.107.refs_1_), channel_id=1, source_target_pairs={{0,16},{1,17},{2,18},{3,19},{4,20},{5,21},{6,22},{7,23},{8,24},{9,... | collective-permute-start | bytes 393224 | tf_op jit(solution)/shard_map/cond/branch_0_fun/ppermute | solution.py:78
  42.6 9.7 %collective-permute-start.13 = (bf16[4,128,128]{2,1,0:T(8,128)(2,1)S(1)}, bf16[4,128,128]{2,1,0:T(8,128)(2,1)S(1)}, u32[]{:S(2)}, u32[]{:S(2)}) collective-permute-start(bf16[4,128,128]{2,1,0:T(8,128)(2,1)S(1)} %get-tuple-element.107.refs_1_), channel_id=1, source_target_pairs={{0,2},{1,3},{2,0},{3,1},{4,6},{5,7},{6,4},{7,5},{8,10},{9,11},{10,... | collective-permute-start | bytes 393224 | tf_op jit(solution)/shard_map/cond/branch_0_fun/ppermute | solution.py:78
  43.9 8.4 %collective-permute-start.14 = (bf16[4,128,128]{2,1,0:T(8,128)(2,1)S(1)}, bf16[4,128,128]{2,1,0:T(8,128)(2,1)S(1)}, u32[]{:S(2)}, u32[]{:S(2)}) collective-permute-start(bf16[4,128,128]{2,1,0:T(8,128)(2,1)S(1)} %get-tuple-element.108.refs_0_), channel_id=1, source_target_pairs={{0,16},{1,17},{2,18},{3,19},{4,20},{5,21},{6,22},{7,23},{8,24},{9,... | collective-permute-start | bytes 393224 | tf_op jit(solution)/shard_map/cond/branch_0_fun/ppermute | solution.py:78
  46.7 6.7 %collective-permute-start.20 = (bf16[16,128,128]{2,1,0:T(8,128)(2,1)S(1)}, bf16[16,128,128]{2,1,0:T(8,128)(2,1)S(1)}, u32[]{:S(2)}, u32[]{:S(2)}) collective-permute-start(bf16[16,128,128]{2,1,0:T(8,128)(2,1)S(1)} %get-tuple-element.115.refs_12_), channel_id=1, source_target_pairs={{0,1},{1,0},{2,3},{3,2},{4,5},{5,4},{6,7},{7,6},{8,9},{9,8},{10,11... | collective-permute-start | bytes 1572872 | tf_op jit(solution)/shard_map/cond/branch_0_fun/ppermute | solution.py:78
  46.8 5.9 %collective-permute-start.16 = (bf16[4,128,128]{2,1,0:T(8,128)(2,1)S(1)}, bf16[4,128,128]{2,1,0:T(8,128)(2,1)S(1)}, u32[]{:S(2)}, u32[]{:S(2)}) collective-permute-start(bf16[4,128,128]{2,1,0:T(8,128)(2,1)S(1)} %collective-permute-done.15.refs_2_), channel_id=1, source_target_pairs={{0,16},{1,17},{2,18},{3,19},{4,20},{5,21},{6,22},{7,23},{8,24},{9,... | collective-permute-start | bytes 393224 | tf_op jit(solution)/shard_map/cond/branch_0_fun/ppermute | solution.py:78
  47.7 5.6 %collective-permute-start.18 = (bf16[4,128,128]{2,1,0:T(8,128)(2,1)S(1)}, bf16[4,128,128]{2,1,0:T(8,128)(2,1)S(1)}, u32[]{:S(2)}, u32[]{:S(2)}) collective-permute-start(bf16[4,128,128]{2,1,0:T(8,128)(2,1)S(1)} %collective-permute-done.17.refs_3_), channel_id=1, source_target_pairs={{0,2},{1,3},{2,0},{3,1},{4,6},{5,7},{6,4},{7,5},{8,10},{9,11},{10,... | collective-permute-start | bytes 393224 | tf_op jit(solution)/shard_map/cond/branch_0_fun/ppermute | solution.py:78
  53.3 2.1 %collective-permute-start.19 = (bf16[16,128,128]{2,1,0:T(8,128)(2,1)S(1)}, bf16[16,128,128]{2,1,0:T(8,128)(2,1)S(1)}, u32[]{:S(2)}, u32[]{:S(2)}) collective-permute-start(bf16[16,128,128]{2,1,0:T(8,128)(2,1)S(1)} %get-tuple-element.112.refs_13_), channel_id=1, source_target_pairs={{0,1},{1,0},{2,3},{3,2},{4,5},{5,4},{6,7},{7,6},{8,9},{9,8},{10,11... | collective-permute-start | bytes 1572872 | tf_op jit(solution)/shard_map/cond/branch_0_fun/ppermute | solution.py:78

commit v2 on v1

--- a/solution.py
+++ b/solution.py
@@ -123,15 +123,15 @@
         self.counts = self.columns * self.groups * self.length
         self.inverse = self.counts + self.columns * self.groups
         self.held = self.inverse + self.length
-        self.place = self.held + 1
+        self.turn = self.held + 1
+        self.place = self.turn + 1
         self.size = self.place + 4
 
     def slot(self, info, group, index):
-        turn = group + self.groups - lax.rem(info[self.place + 1], self.groups)
-        return self.groups * index + lax.rem(turn, self.groups)
-
-
-def table_kernel(grid, table, owners, source, out, level, fetched, seen, sem):
+        return self.groups * index + lax.rem(group + info[self.turn], self.groups)
+
+
+def table_kernel(grid, table, owners, source, out, level, fetched, seen, turns, sem):
     copy = pltpu.make_async_copy(source, fetched, sem)
     copy.start()
     place = grid.place()
@@ -144,12 +144,28 @@
     column_mine = place[2] * grid.core + place[3]
     mine = column_mine * table.groups + lax.div(place[0], table.shares)
 
+    def count(block, carry):
+        owner = owners[block]
+        seen[owner] = seen[owner] + 1
+        return carry
+
+    lax.fori_loop(0, owners.shape[0], count, 0, unroll=8)
+    out[table.held] = seen[place[1] * table.columns + column_mine]
+    for column in range(table.columns):
+        turn = 0
+        for high in range(grid.high):
+            owner = high * table.columns + column
+            turns[owner] = turn
+            turn = (turn + seen[owner]) & (table.groups - 1)
+            seen[owner] = 0
+    out[table.turn] = (table.groups - turns[place[1] * table.columns + column_mine]) & (table.groups - 1)
+
     def step(block, carry):
         owner = owners[block]
         rank = seen[owner]
         seen[owner] = rank + 1
         column, high = owner & (table.columns - 1), owner >> log2(table.columns)
-        group, index = (rank + high) & (table.groups - 1), rank >> log2(table.groups)
+        group, index = (rank + turns[owner]) & (table.groups - 1), rank >> log2(table.groups)
         part = column * table.groups + group
         at = out[table.counts + part]
         out[table.counts + part] = at + 1
@@ -162,7 +178,6 @@
         return carry
 
     lax.fori_loop(0, owners.shape[0], step, 0, unroll=8)
-    out[table.held] = seen[place[1] * table.columns + column_mine]
     most = out[table.counts]
     for part in range(1, table.columns * table.groups):
         most = jnp.maximum(most, out[table.counts + part])
@@ -280,27 +295,30 @@
         updated[index] = (weights - 0.01 * (moved + 0.1 * weights)).astype(BF16)
 
 
-def refresh(gradient, left_stat, right_stat, left, right, pairs):
+def refresh(short, gradient, left_stat, right_stat, left, right, pairs):
     iterates = []
     for dims, stat, basis in ((NT, left_stat, left), (TN, right_stat, right)):
         for index, slot in pairs:
             gram = dot(gradient[index], gradient[index], dims)
             power = product(as_left(0.95 * stat[slot] + 0.05 * gram), as_right(basis[slot]))
             iterates.append(power / (jnp.sqrt(jnp.sum(power * power)) + 1e-06))
-    for _ in range(NS_ITERS):
+
+    def step(_, iterates):
         squares = [product(as_left(x, 0), as_right(x), TN) for x in iterates]
-        iterates = [
+        return [
             1.5 * x - 0.5 * product(as_left(x), as_right(square))
             for x, square in zip(iterates, squares, strict=True)
         ]
+
+    iterates = lax.fori_loop(0, NS_ITERS, step, iterates, unroll=1 if short else NS_ITERS)
     return iterates[: len(pairs)], iterates[len(pairs) :]
 
 
-def own_kernel(table, info, gradient, turned, left_plain, stat_left, stat_right, left, right, *refs):
+def own_kernel(table, short, info, gradient, turned, left_plain, stat_left, stat_right, left, right, *refs):
     outs, (held, sem) = refs[:3], refs[3:]
     group = lax.div(info[table.place], table.shares)
     pairs = [(index, table.slot(info, group, index)) for index in range(table.each)]
-    new_left, new_right = refresh(gradient, stat_left, stat_right, left, right, pairs)
+    new_left, new_right = refresh(short, gradient, stat_left, stat_right, left, right, pairs)
     copies = []
     for index, slot in pairs:
         live = slot < info[table.held]
@@ -315,30 +333,37 @@
         copy.wait()
 
 
-def others_kernel(table, info, *refs):
+def others_kernel(grid, table, layout, short, info, *refs):
     count = table.groups - 1
-    gradients, bases, (left_out, right_out) = refs[:count], refs[count : count + 4], refs[-2:]
+    gradients, bases, packed = refs[:count], refs[count : count + 4], refs[count + 4]
+    weights, left_out, right_out, sem = refs[-4:]
+
+    def place(act):
+        place_blocks(grid, table, layout, 0, info, [packed], weights, sem, act)
+
+    place(lambda copy: copy.start())
     group = lax.div(info[table.place], table.shares)
     for dg, gradient in enumerate(gradients, 1):
         pairs = [(index, table.slot(info, group ^ dg, index)) for index in range(table.each)]
-        new_left, new_right = refresh(gradient, *bases, pairs)
+        new_left, new_right = refresh(short, gradient, *bases, pairs)
         for index, slot in pairs:
             at = (dg - 1) * table.each + index
             live = slot < info[table.held]
             left_out[at] = jnp.where(live, new_left[index], bases[2][slot])
             right_out[at] = jnp.where(live, new_right[index], bases[3][slot])
-
-
-def finish_kernel(grid, table, layout, info, correction, *refs):
+    place(lambda copy: copy.wait())
+
+
+def finish_kernel(grid, table, early_layout, layout, info, correction, *refs):
     count = table.groups - 1
     gradients, refs = refs[:count], refs[count:]
     (rot_old, second, left_plain, left_turned, right_tall, right_turned) = refs[:6]
-    new_left, new_right, across, *packed = refs[6 : 9 + len(layout)]
-    direction, left_out, right_out, weights, held, sem = refs[9 + len(layout) :]
+    new_left, new_right, packed, across = refs[6:10]
+    direction, left_out, right_out, weights, held, sem = refs[10:]
 
     def place(act):
-        place_blocks(grid, table, layout[:1], 1, info, [across], weights, sem, act)
-        place_blocks(grid, table, layout, 0, info, packed, weights, sem, act)
+        place_blocks(grid, table, layout, 0, info, [packed], weights, sem, act)
+        place_blocks(grid, table, early_layout, 1, info, [across], weights, sem, act)
 
     place(lambda copy: copy.start())
     group = lax.div(info[table.place], table.shares)
@@ -445,7 +470,7 @@
         ),
         in_specs=[SMEM, HBM],
         out_specs=(SMEM, SMEM, VMEM),
-        scratch_shapes=[pltpu.SMEM((grid.owners,), jnp.int32), pltpu.SemaphoreType.DMA],
+        scratch_shapes=[pltpu.SMEM((grid.owners,), jnp.int32)] * 2 + [pltpu.SemaphoreType.DMA],
         compiler_params=pltpu.CompilerParams(vmem_limit_bytes=VMEM_LIMIT),
     )(
         pltpu.with_memory_space_constraint(owners, pltpu.SMEM),
@@ -482,6 +507,7 @@
     slots, size = master.shape[:2]
     blocks = own.shape[0]
     rows = size // table.shares
+    short = room > table.rooms[1]
     chain = Chain()
     correction = 1.0 - jnp.power(jnp.float32(0.95), step_count.astype(F32))
     share = shape((table.each, rows, size), BF16)
@@ -570,7 +596,7 @@
     bases = (stat_left, stat_right, basis_left, basis_right)
     whole = pltpu.HBM((slots, size, size), F32)
     done = chain.call(
-        functools.partial(own_kernel, table),
+        functools.partial(own_kernel, table, short),
         (info,),
         (gradient, turned, left_plain, *bases),
         [whole] * 3,
@@ -586,35 +612,40 @@
         scratch=(pltpu.VMEM((table.length, rows, size), BF16),),
     )
     early, late = gather_plane(held)
-    layout = [[(place, cuts[piece], cuts[piece + 1]) for _, place, piece in part] for part in (early, late)]
-    packed = [pack(early)]
+    early_layout, late_layout = (
+        [[(place, cuts[piece], cuts[piece + 1]) for _, place, piece in part]] for part in (early, late)
+    )
+    early = pack(early)
     others_state = shape(((table.groups - 1) * table.each, size, size), F32)
-    new_bases = chain.call(
-        functools.partial(others_kernel, table),
+    weights = pltpu.HBM((blocks, size, size), BF16)
+    weights_early, new_left, new_right = chain.call(
+        functools.partial(others_kernel, grid, table, early_layout, short),
         (info,),
-        (*others, *bases),
-        [others_state] * 2,
+        (*others, *bases, early),
+        [weights, others_state, others_state],
         400 * passes,
-    )
-    packed.append(pack(late))
-    across = [grid.swap(array, core=1) for array in packed]
+        scratch=(pltpu.SemaphoreType.DMA,),
+        specs=[HBM, VMEM, VMEM],
+    )
+    early_across = grid.swap(early, core=1)
+    late = pack(late)
+    late_across = grid.swap(late, core=1)
     prepared = (rot_old, second, left_plain, left_turned, right_tall, right_turned)
-    weights = pltpu.HBM((blocks, size, size), BF16)
     direction, left_new, right_new, weights_own = chain.call(
-        functools.partial(finish_kernel, grid, table, layout),
+        functools.partial(finish_kernel, grid, table, early_layout, late_layout),
         (info, correction),
-        (*others, *prepared, *new_bases, across[0], *packed),
+        (*others, *prepared, new_left, new_right, late, early_across),
         [whole] * 3 + [weights],
         100 * passes,
         scratch=(pltpu.VMEM(others_state.shape, F32), pltpu.SemaphoreType.DMA),
         specs=[HBM] * 4,
         moved=1,
-        reuse=done,
+        reuse=(*done, weights_early),
     )
     (weights_all,) = chain.call(
-        functools.partial(weights_kernel, grid, table, layout[1:]),
+        functools.partial(weights_kernel, grid, table, late_layout),
         (info,),
-        across[1:],
+        (late_across,),
         [weights],
         scratch=(pltpu.SemaphoreType.DMA,),
         specs=[HBM],

time: 57.1 us -> 57.3 us (level)
  waiting for transfers between devices: 17.4 us -> 18 us
    ppermute x22, waiting for transfers between devices: 17.4 us -> 18 us  [swap(): return lax.ppermute(array, AXES, pairs)]
  transfers between devices with their start and end apart: 22 -> 22, of which waited for: 14 -> 12; matrix products, arithmetic and copies ran while one was open for 0% -> 0% of each run, Pallas kernels for 21% -> 21%
where the time goes in v2:
time: 57.3 us; the launch traced here: 57.4 us
  starting transfers between devices  22.1 us (39%)
  waiting for transfers between devices  18 us (31%)
  Pallas kernels  14.6 us (25%)
  loops' own time  1.11 us (2%)
  between operations  0.84 us (1%)
  local copies, waits for them, and re-layouts  0.69 us (1%)
    ppermute x22, starting transfers between devices, swap(): return lax.ppermute(array, AXES, pairs)  22.1 us
    ppermute x22, waiting for transfers between devices, swap(): return lax.ppermute(array, AXES, pairs)  18 us
    pallas_call x13, Pallas kernels, call(): pl.pallas_call(run, out_shape=(*outs, shape((8, 128), F32)), in_specs=[SM...  12.7 us
    pallas_call x1, Pallas kernels, body(): pl.pallas_call(functools.partial(table_kernel, grid, table), out_shape=(p...  1.96 us
  transfers between devices with their start and end apart: 22, of which 12 were waited for; matrix products, arithmetic and copies ran while one was open for 0% of the time, Pallas kernels for 21%

profile of v2, /device:TPU:0, one launch (start us, length us, event | category | flops | bytes accessed | tf_op | source)
XLA Modules:
  0.0 57.4 jit_solution(6053886700004883650)
XLA Ops:
  1.2 0.7 %copy-done = s32[48]{0:T(128)S(1)} copy-done((s32[48]{0:T(128)S(1)}, s32[48]{0:T(128)}, u32[]{:S(2)}) %copy-start) | copy-done | bytes 216
  1.8 2.0 %shard_map.129 = (s32[122]{0:T(128)S(4)}, s32[1]{0:T(128)S(4)}, bf16[48,128,128]{2,1,0:T(8,128)(2,1)S(1)}) custom-call(s32[48]{0:T(128)S(1)} %copy-done, bf16[48,128,128]{2,1,0:T(8,128)(2,1)} %bitcast.3), custom_call_target="tpu_custom_call" | custom-call | tf_op jit(solution)/shard_map/pallas_call | solution.py:464
  3.8 0.6 %collective-permute-done.63 = bf16[48,128,128]{2,1,0:T(8,128)(2,1)S(1)} collective-permute-done((bf16[48,128,128]{2,1,0:T(8,128)(2,1)}, bf16[48,128,128]{2,1,0:T(8,128)(2,1)S(1)}, u32[]{:S(2)}, u32[]{:S(2)}) %collective-permute-start.63) | collective-permute-done | bytes 1572896 | tf_op jit(solution)/shard_map/ppermute | solution.py:78
  4.4 52.8 %conditional.1 = (bf16[48,128,128]{2,1,0:T(8,128)(2,1)}, f32[6,128,128]{2,1,0:T(8,128)}, f32[6,128,128]{2,1,0:T(8,128)}, f32[6,128,128]{2,1,0:T(8,128)}) conditional(s32[]{:T(128)} %bitcast.1, (s32[1]{0:T(128)}, s32[122]{0:T(128)S(4)}, bf16[48,128,128]{2,1,0:T(8,128)(2,1)S(1)}, bf16[48,128,128]{2,1,0:T(8,128)(2,1)S(1)}, ...), branch_computations={%region_0.0_spmd, %region_1.0_spmd, %region_2.0_spmd} | conditional | flops 11702108160 | bytes 47088604 | solution.py:480
  4.9 2.9 %collective-permute-start.1 = (bf16[4,128,128]{2,1,0:T(8,128)(2,1)S(1)}, bf16[4,128,128]{2,1,0:T(8,128)(2,1)S(1)}, u32[]{:S(2)}, u32[]{:S(2)}) collective-permute-start(bf16[4,128,128]{2,1,0:T(8,128)(2,1)S(1)} %get-tuple-element.74), channel_id=1, source_target_pairs={{0,2},{1,3},{2,0},{3,1},{4,6},{5,7},{6,4},{7,5},{8,10},{9,11},{10,... | collective-permute-start | bytes 393224 | tf_op jit(solution)/shard_map/cond/branch_0_fun/ppermute | solution.py:78
  7.9 1.5 %collective-permute-start.2 = (bf16[4,128,128]{2,1,0:T(8,128)(2,1)S(1)}, bf16[4,128,128]{2,1,0:T(8,128)(2,1)S(1)}, u32[]{:S(2)}, u32[]{:S(2)}) collective-permute-start(bf16[4,128,128]{2,1,0:T(8,128)(2,1)S(1)} %get-tuple-element.75), channel_id=1, source_target_pairs={{0,16},{1,17},{2,18},{3,19},{4,20},{5,21},{6,22},{7,23},{8,24},{9,... | collective-permute-start | bytes 393224 | tf_op jit(solution)/shard_map/cond/branch_0_fun/ppermute | solution.py:78
  10.0 1.8 %collective-permute-done.1.refs_2_ = bf16[4,128,128]{2,1,0:T(8,128)(2,1)S(1)} collective-permute-done((bf16[4,128,128]{2,1,0:T(8,128)(2,1)S(1)}, bf16[4,128,128]{2,1,0:T(8,128)(2,1)S(1)}, u32[]{:S(2)}, u32[]{:S(2)}) %collective-permute-start.1) | collective-permute-done | bytes 131104 | tf_op jit(solution)/shard_map/cond/branch_0_fun/ppermute | solution.py:78
  11.7 2.5 %collective-permute-done.2.refs_3_ = bf16[4,128,128]{2,1,0:T(8,128)(2,1)S(1)} collective-permute-done((bf16[4,128,128]{2,1,0:T(8,128)(2,1)S(1)}, bf16[4,128,128]{2,1,0:T(8,128)(2,1)S(1)}, u32[]{:S(2)}, u32[]{:S(2)}) %collective-permute-start.2) | collective-permute-done | bytes 131104 | tf_op jit(solution)/shard_map/cond/branch_0_fun/ppermute | solution.py:78
  14.3 1.6 %collective-permute-start.3 = (bf16[4,128,128]{2,1,0:T(8,128)(2,1)S(1)}, bf16[4,128,128]{2,1,0:T(8,128)(2,1)S(1)}, u32[]{:S(2)}, u32[]{:S(2)}) collective-permute-start(bf16[4,128,128]{2,1,0:T(8,128)(2,1)S(1)} %get-tuple-element.77), channel_id=1, source_target_pairs={{0,16},{1,17},{2,18},{3,19},{4,20},{5,21},{6,22},{7,23},{8,24},{9,... | collective-permute-start | bytes 393224 | tf_op jit(solution)/shard_map/cond/branch_0_fun/ppermute | solution.py:78
  16.4 0.5 branch_0_fun.15
  17.0 2.3 %collective-permute-done.3.refs_3_ = bf16[4,128,128]{2,1,0:T(8,128)(2,1)S(1)} collective-permute-done((bf16[4,128,128]{2,1,0:T(8,128)(2,1)S(1)}, bf16[4,128,128]{2,1,0:T(8,128)(2,1)S(1)}, u32[]{:S(2)}, u32[]{:S(2)}) %collective-permute-start.3) | collective-permute-done | bytes 131104 | tf_op jit(solution)/shard_map/cond/branch_0_fun/ppermute | solution.py:78
  19.4 1.5 %collective-permute-done.5.refs_6_ = bf16[4,128,128]{2,1,0:T(8,128)(2,1)S(1)} collective-permute-done((bf16[4,128,128]{2,1,0:T(8,128)(2,1)S(1)}, bf16[4,128,128]{2,1,0:T(8,128)(2,1)S(1)}, u32[]{:S(2)}, u32[]{:S(2)}) %collective-permute-start.5) | collective-permute-done | bytes 131104 | tf_op jit(solution)/shard_map/cond/branch_0_fun/ppermute | solution.py:78
  21.0 3.7 %collective-permute-start.6 = (bf16[3,128,128]{2,1,0:T(8,128)(2,1)S(1)}, bf16[3,128,128]{2,1,0:T(8,128)(2,1)S(1)}, u32[]{:S(2)}, u32[]{:S(2)}) collective-permute-start(bf16[3,128,128]{2,1,0:T(8,128)(2,1)S(1)} %get-tuple-element.86), channel_id=1, source_target_pairs={{0,12},{1,13},{2,14},{3,15},{4,8},{5,9},{6,10},{7,11},{8,4},{9,5},... | collective-permute-start | bytes 294920 | tf_op jit(solution)/shard_map/cond/branch_0_fun/ppermute | solution.py:78
  24.7 0.8 %collective-permute-start.8 = (bf16[3,128,128]{2,1,0:T(8,128)(2,1)S(1)}, bf16[3,128,128]{2,1,0:T(8,128)(2,1)S(1)}, u32[]{:S(2)}, u32[]{:S(2)}) collective-permute-start(bf16[3,128,128]{2,1,0:T(8,128)(2,1)S(1)} %get-tuple-element.88), channel_id=1, source_target_pairs={{0,4},{1,5},{2,6},{3,7},{4,0},{5,1},{6,2},{7,3},{8,12},{9,13},{10,... | collective-permute-start | bytes 294920 | tf_op jit(solution)/shard_map/cond/branch_0_fun/ppermute | solution.py:78
  26.2 1.4 %collective-permute-done.6.refs_0_ = bf16[3,128,128]{2,1,0:T(8,128)(2,1)S(1)} collective-permute-done((bf16[3,128,128]{2,1,0:T(8,128)(2,1)S(1)}, bf16[3,128,128]{2,1,0:T(8,128)(2,1)S(1)}, u32[]{:S(2)}, u32[]{:S(2)}) %collective-permute-start.6) | collective-permute-done | bytes 98336 | tf_op jit(solution)/shard_map/cond/branch_0_fun/ppermute | solution.py:78
  27.6 3.4 %collective-permute-done.7.refs_1_ = bf16[3,128,128]{2,1,0:T(8,128)(2,1)S(1)} collective-permute-done((bf16[3,128,128]{2,1,0:T(8,128)(2,1)S(1)}, bf16[3,128,128]{2,1,0:T(8,128)(2,1)S(1)}, u32[]{:S(2)}, u32[]{:S(2)}) %collective-permute-start.7) | collective-permute-done | bytes 98336 | tf_op jit(solution)/shard_map/cond/branch_0_fun/ppermute | solution.py:78
  31.1 0.8 %branch_0_fun.18 = (bf16[3,128,128]{2,1,0:T(8,128)(2,1)S(1)}, f32[3,128,128]{2,1,0:T(8,128)S(1)}, bf16[3,128,128]{2,1,0:T(8,128)(2,1)S(1)}, f32[8,128]{1,0:T(8,128)S(1)}) custom-call(s32[122]{0:T(128)S(4)} %get-tuple-element.66.refs_0_, f32[1]{0:T(128)S(6)} %sub.6.refs_1_, bf16[3,128,128]{2,1,0:T(8,128)(2,1)S(1)} %get-tuple-element.91.refs_2_, ...), custom_call_target="tpu_custom_call" | custom-call | flops 176160768 | bytes 3637248 | tf_op jit(solution)/shard_map/cond/branch_0_fun/pallas_call | solution.py:43
  31.9 1.8 %collective-permute-start.11 = (bf16[3,128,128]{2,1,0:T(8,128)(2,1)S(1)}, bf16[3,128,128]{2,1,0:T(8,128)(2,1)S(1)}, u32[]{:S(2)}, u32[]{:S(2)}) collective-permute-start(bf16[3,128,128]{2,1,0:T(8,128)(2,1)S(1)} %get-tuple-element.100.refs_4_), channel_id=1, source_target_pairs={{0,12},{1,13},{2,14},{3,15},{4,8},{5,9},{6,10},{7,11},{8,4},{9,5},... | collective-permute-start | bytes 294920 | tf_op jit(solution)/shard_map/cond/branch_0_fun/ppermute | solution.py:78
  33.7 0.6 %collective-permute-start.10 = (bf16[3,128,128]{2,1,0:T(8,128)(2,1)S(1)}, bf16[3,128,128]{2,1,0:T(8,128)(2,1)S(1)}, u32[]{:S(2)}, u32[]{:S(2)}) collective-permute-start(bf16[3,128,128]{2,1,0:T(8,128)(2,1)S(1)} %get-tuple-element.100.refs_4_), channel_id=1, source_target_pairs={{0,8},{1,9},{2,10},{3,11},{4,12},{5,13},{6,14},{7,15},{8,0},{9,1},... | collective-permute-start | bytes 294920 | tf_op jit(solution)/shard_map/cond/branch_0_fun/ppermute | solution.py:78
  34.3 2.1 %collective-permute-start.9 = (bf16[3,128,128]{2,1,0:T(8,128)(2,1)S(1)}, bf16[3,128,128]{2,1,0:T(8,128)(2,1)S(1)}, u32[]{:S(2)}, u32[]{:S(2)}) collective-permute-start(bf16[3,128,128]{2,1,0:T(8,128)(2,1)S(1)} %get-tuple-element.100.refs_4_), channel_id=1, source_target_pairs={{0,4},{1,5},{2,6},{3,7},{4,0},{5,1},{6,2},{7,3},{8,12},{9,13},{10,... | collective-permute-start | bytes 294920 | tf_op jit(solution)/shard_map/cond/branch_0_fun/ppermute | solution.py:78
  36.4 4.0 %branch_0_fun.19 = (f32[6,128,128]{2,1,0:T(8,128)}, f32[6,128,128]{2,1,0:T(8,128)}, f32[6,128,128]{2,1,0:T(8,128)}, f32[8,128]{1,0:T(8,128)S(1)}) custom-call(s32[122]{0:T(128)S(4)} %get-tuple-element.66.refs_0_, bf16[3,128,128]{2,1,0:T(8,128)(2,1)S(1)} %get-tuple-element.101.refs_1_, f32[3,128,128]{2,1,0:T(8,128)S(1)} %get-tuple-element.102.refs_2_, ...), custom_call_target="tpu_custom_call" | custom-call | flops 5033164800 | bytes 3440640 | tf_op jit(solution)/shard_map/cond/branch_0_fun/pallas_call | solution.py:43
  40.4 1.2 %collective-permute-done.12.refs_5_.refs_1_.refs_2_ = bf16[3,128,128]{2,1,0:T(8,128)(2,1)S(1)} collective-permute-done((bf16[3,128,128]{2,1,0:T(8,128)(2,1)S(1)}, bf16[3,128,128]{2,1,0:T(8,128)(2,1)S(1)}, u32[]{:S(2)}, u32[]{:S(2)}) %collective-permute-start.12) | collective-permute-done | bytes 98336 | tf_op jit(solution)/shard_map/cond/branch_0_fun/ppermute | solution.py:78
  41.7 0.9 %collective-permute-start.17 = (bf16[4,128,128]{2,1,0:T(8,128)(2,1)S(1)}, bf16[4,128,128]{2,1,0:T(8,128)(2,1)S(1)}, u32[]{:S(2)}, u32[]{:S(2)}) collective-permute-start(bf16[4,128,128]{2,1,0:T(8,128)(2,1)S(1)} %get-tuple-element.107.refs_1_), channel_id=1, source_target_pairs={{0,16},{1,17},{2,18},{3,19},{4,20},{5,21},{6,22},{7,23},{8,24},{9,... | collective-permute-start | bytes 393224 | tf_op jit(solution)/shard_map/cond/branch_0_fun/ppermute | solution.py:78
  42.8 1.9 %collective-permute-start.13 = (bf16[4,128,128]{2,1,0:T(8,128)(2,1)S(1)}, bf16[4,128,128]{2,1,0:T(8,128)(2,1)S(1)}, u32[]{:S(2)}, u32[]{:S(2)}) collective-permute-start(bf16[4,128,128]{2,1,0:T(8,128)(2,1)S(1)} %get-tuple-element.107.refs_1_), channel_id=1, source_target_pairs={{0,2},{1,3},{2,0},{3,1},{4,6},{5,7},{6,4},{7,5},{8,10},{9,11},{10,... | collective-permute-start | bytes 393224 | tf_op jit(solution)/shard_map/cond/branch_0_fun/ppermute | solution.py:78
  44.6 1.1 %collective-permute-start.14 = (bf16[4,128,128]{2,1,0:T(8,128)(2,1)S(1)}, bf16[4,128,128]{2,1,0:T(8,128)(2,1)S(1)}, u32[]{:S(2)}, u32[]{:S(2)}) collective-permute-start(bf16[4,128,128]{2,1,0:T(8,128)(2,1)S(1)} %get-tuple-element.108.refs_0_), channel_id=1, source_target_pairs={{0,16},{1,17},{2,18},{3,19},{4,20},{5,21},{6,22},{7,23},{8,24},{9,... | collective-permute-start | bytes 393224 | tf_op jit(solution)/shard_map/cond/branch_0_fun/ppermute | solution.py:78
  45.8 0.9 %collective-permute-done.17.refs_3_ = bf16[4,128,128]{2,1,0:T(8,128)(2,1)S(1)} collective-permute-done((bf16[4,128,128]{2,1,0:T(8,128)(2,1)S(1)}, bf16[4,128,128]{2,1,0:T(8,128)(2,1)S(1)}, u32[]{:S(2)}, u32[]{:S(2)}) %collective-permute-start.17) | collective-permute-done | bytes 131104 | tf_op jit(solution)/shard_map/cond/branch_0_fun/ppermute | solution.py:78
  46.7 0.9 %collective-permute-done.15.refs_2_ = bf16[4,128,128]{2,1,0:T(8,128)(2,1)S(1)} collective-permute-done((bf16[4,128,128]{2,1,0:T(8,128)(2,1)S(1)}, bf16[4,128,128]{2,1,0:T(8,128)(2,1)S(1)}, u32[]{:S(2)}, u32[]{:S(2)}) %collective-permute-start.15) | collective-permute-done | bytes 131104 | tf_op jit(solution)/shard_map/cond/branch_0_fun/ppermute | solution.py:78
  47.9 1.1 %collective-permute-start.16 = (bf16[4,128,128]{2,1,0:T(8,128)(2,1)S(1)}, bf16[4,128,128]{2,1,0:T(8,128)(2,1)S(1)}, u32[]{:S(2)}, u32[]{:S(2)}) collective-permute-start(bf16[4,128,128]{2,1,0:T(8,128)(2,1)S(1)} %collective-permute-done.15.refs_2_), channel_id=1, source_target_pairs={{0,16},{1,17},{2,18},{3,19},{4,20},{5,21},{6,22},{7,23},{8,24},{9,... | collective-permute-start | bytes 393224 | tf_op jit(solution)/shard_map/cond/branch_0_fun/ppermute | solution.py:78
  49.0 3.3 %branch_0_fun.22 = (bf16[48,128,128]{2,1,0:T(8,128)(2,1)}, f32[3,128,128]{2,1,0:T(8,128)S(1)}, f32[3,128,128]{2,1,0:T(8,128)S(1)}, f32[8,128]{1,0:T(8,128)S(1)}) custom-call(s32[122]{0:T(128)S(4)} %get-tuple-element.66.refs_0_, bf16[3,128,128]{2,1,0:T(8,128)(2,1)S(1)} %collective-permute-done.12.refs_5_.refs_1_.refs_2_, f32[6,128,128]{2,1,0:T(8,128)S(1)} %copy-done.8, ...), custom_call_target="tpu_custom_call" | custom-call | flops 5033164800 | bytes 4161536 | tf_op jit(solution)/shard_map/cond/branch_0_fun/pallas_call | solution.py:43
  52.4 1.3 %collective-permute-done.18.refs_3_ = bf16[4,128,128]{2,1,0:T(8,128)(2,1)S(1)} collective-permute-done((bf16[4,128,128]{2,1,0:T(8,128)(2,1)S(1)}, bf16[4,128,128]{2,1,0:T(8,128)(2,1)S(1)}, u32[]{:S(2)}, u32[]{:S(2)}) %collective-permute-start.18) | collective-permute-done | bytes 131104 | tf_op jit(solution)/shard_map/cond/branch_0_fun/ppermute | solution.py:78
  53.8 1.8 %branch_0_fun.24 = (f32[6,128,128]{2,1,0:T(8,128)}, f32[6,128,128]{2,1,0:T(8,128)}, f32[6,128,128]{2,1,0:T(8,128)}, bf16[48,128,128]{2,1,0:T(8,128)(2,1)}, f32[8,128]{1,0:T(8,128)S(1)}) custom-call(s32[122]{0:T(128)S(4)} %get-tuple-element.66.refs_0_, f32[1]{0:T(128)S(6)} %sub.6.refs_1_, ...), custom_call_target="tpu_custom_call", output_to_operand_aliasing={{0}: (14, {}), {1}: (15, {}), {2}: (16, {}), {3}: (17, {})} | custom-call | flops 1258291200 | bytes 1 | tf_op jit(solution)/shard_map/cond/branch_0_fun/pallas_call | solution.py:43
  55.6 1.3 %branch_0_fun.25 = (bf16[48,128,128]{2,1,0:T(8,128)(2,1)}, f32[8,128]{1,0:T(8,128)}) custom-call(s32[122]{0:T(128)S(4)} %get-tuple-element.66.refs_0_, bf16[16,128,128]{2,1,0:T(8,128)(2,1)S(1)} %collective-permute-done.19.refs_1_, f32[8,128]{1,0:T(8,128)S(1)} %get-tuple-element.121.refs_2_, ...), custom_call_target="tpu_custom_call", output_to_operand_aliasing={{0}: (3, {})} | custom-call | bytes 1 | tf_op jit(solution)/shard_map/cond/branch_0_fun/pallas_call | solution.py:43
  (43 shorter events, 3.2 us)
Async XLA Ops:
  0.6 3.8 %collective-permute-start.63 = (bf16[48,128,128]{2,1,0:T(8,128)(2,1)}, bf16[48,128,128]{2,1,0:T(8,128)(2,1)S(1)}, u32[]{:S(2)}, u32[]{:S(2)}) collective-permute-start(bf16[48,128,128]{2,1,0:T(8,128)(2,1)} %bitcast.2), channel_id=1, source_target_pairs={{0,1},{1,0},{2,3},{3,2},{4,5},{5,4},{6,7},{7,6},{8,9},{9,8},{10,11... | collective-permute-start | bytes 4718600 | tf_op jit(solution)/shard_map/ppermute | solution.py:78
  1.2 0.7 %copy-start = (s32[48]{0:T(128)S(1)}, s32[48]{0:T(128)}, u32[]{:S(2)}) copy-start(s32[48]{0:T(128)} %owners.1) | copy-start | bytes 580
  1.8 2.6 %copy-start.1 = (f32[6,128,128]{2,1,0:T(8,128)S(1)}, f32[6,128,128]{2,1,0:T(8,128)}, u32[]{:S(2)}) copy-start(f32[6,128,128]{2,1,0:T(8,128)} %param.18) | copy-start | bytes 1179652
  1.8 2.6 %copy-start.2 = (f32[6,128,128]{2,1,0:T(8,128)S(1)}, f32[6,128,128]{2,1,0:T(8,128)}, u32[]{:S(2)}) copy-start(f32[6,128,128]{2,1,0:T(8,128)} %param.16) | copy-start | bytes 1179652
  1.8 2.6 %copy-start.3 = (f32[6,128,128]{2,1,0:T(8,128)S(1)}, f32[6,128,128]{2,1,0:T(8,128)}, u32[]{:S(2)}) copy-start(f32[6,128,128]{2,1,0:T(8,128)} %param.17) | copy-start | bytes 1179652
  1.8 2.6 %copy-start.4 = (f32[6,128,128]{2,1,0:T(8,128)S(1)}, f32[6,128,128]{2,1,0:T(8,128)}, u32[]{:S(2)}) copy-start(f32[6,128,128]{2,1,0:T(8,128)} %param.21) | copy-start | bytes 1179652
  4.4 12.0 %copy-start.5 = (f32[6,128,128]{2,1,0:T(8,128)S(1)}, f32[6,128,128]{2,1,0:T(8,128)}, u32[]{:S(2)}) copy-start(f32[6,128,128]{2,1,0:T(8,128)} %get-tuple-element.83.refs_2_.refs_7_.refs_5_) | copy-start | bytes 1179652 | tf_op jit(solution)/shard_map/cond
  4.9 6.8 %collective-permute-start.1 = (bf16[4,128,128]{2,1,0:T(8,128)(2,1)S(1)}, bf16[4,128,128]{2,1,0:T(8,128)(2,1)S(1)}, u32[]{:S(2)}, u32[]{:S(2)}) collective-permute-start(bf16[4,128,128]{2,1,0:T(8,128)(2,1)S(1)} %get-tuple-element.74), channel_id=1, source_target_pairs={{0,2},{1,3},{2,0},{3,1},{4,6},{5,7},{6,4},{7,5},{8,10},{9,11},{10,... | collective-permute-start | bytes 393224 | tf_op jit(solution)/shard_map/cond/branch_0_fun/ppermute | solution.py:78
  7.9 6.4 %collective-permute-start.2 = (bf16[4,128,128]{2,1,0:T(8,128)(2,1)S(1)}, bf16[4,128,128]{2,1,0:T(8,128)(2,1)S(1)}, u32[]{:S(2)}, u32[]{:S(2)}) collective-permute-start(bf16[4,128,128]{2,1,0:T(8,128)(2,1)S(1)} %get-tuple-element.75), channel_id=1, source_target_pairs={{0,16},{1,17},{2,18},{3,19},{4,20},{5,21},{6,22},{7,23},{8,24},{9,... | collective-permute-start | bytes 393224 | tf_op jit(solution)/shard_map/cond/branch_0_fun/ppermute | solution.py:78
  9.4 7.6 %collective-permute-start = (bf16[4,128,128]{2,1,0:T(8,128)(2,1)S(1)}, bf16[4,128,128]{2,1,0:T(8,128)(2,1)S(1)}, u32[]{:S(2)}, u32[]{:S(2)}) collective-permute-start(bf16[4,128,128]{2,1,0:T(8,128)(2,1)S(1)} %get-tuple-element.71), channel_id=1, source_target_pairs={{0,2},{1,3},{2,0},{3,1},{4,6},{5,7},{6,4},{7,5},{8,10},{9,11},{10,... | collective-permute-start | bytes 393224 | tf_op jit(solution)/shard_map/cond/branch_0_fun/ppermute | solution.py:78
  9.9 7.1 %collective-permute-start.4 = (bf16[4,128,128]{2,1,0:T(8,128)(2,1)S(1)}, bf16[4,128,128]{2,1,0:T(8,128)(2,1)S(1)}, u32[]{:S(2)}, u32[]{:S(2)}) collective-permute-start(bf16[4,128,128]{2,1,0:T(8,128)(2,1)S(1)} %get-tuple-element.79), channel_id=1, source_target_pairs={{0,16},{1,17},{2,18},{3,19},{4,20},{5,21},{6,22},{7,23},{8,24},{9,... | collective-permute-start | bytes 393224 | tf_op jit(solution)/shard_map/cond/branch_0_fun/ppermute | solution.py:78
  14.3 5.0 %collective-permute-start.3 = (bf16[4,128,128]{2,1,0:T(8,128)(2,1)S(1)}, bf16[4,128,128]{2,1,0:T(8,128)(2,1)S(1)}, u32[]{:S(2)}, u32[]{:S(2)}) collective-permute-start(bf16[4,128,128]{2,1,0:T(8,128)(2,1)S(1)} %get-tuple-element.77), channel_id=1, source_target_pairs={{0,16},{1,17},{2,18},{3,19},{4,20},{5,21},{6,22},{7,23},{8,24},{9,... | collective-permute-start | bytes 393224 | tf_op jit(solution)/shard_map/cond/branch_0_fun/ppermute | solution.py:78
  15.9 5.0 %collective-permute-start.5 = (bf16[4,128,128]{2,1,0:T(8,128)(2,1)S(1)}, bf16[4,128,128]{2,1,0:T(8,128)(2,1)S(1)}, u32[]{:S(2)}, u32[]{:S(2)}) collective-permute-start(bf16[4,128,128]{2,1,0:T(8,128)(2,1)S(1)} %get-tuple-element.80), channel_id=1, source_target_pairs={{0,2},{1,3},{2,0},{3,1},{4,6},{5,7},{6,4},{7,5},{8,10},{9,11},{10,... | collective-permute-start | bytes 393224 | tf_op jit(solution)/shard_map/cond/branch_0_fun/ppermute | solution.py:78
  21.0 6.6 %collective-permute-start.6 = (bf16[3,128,128]{2,1,0:T(8,128)(2,1)S(1)}, bf16[3,128,128]{2,1,0:T(8,128)(2,1)S(1)}, u32[]{:S(2)}, u32[]{:S(2)}) collective-permute-start(bf16[3,128,128]{2,1,0:T(8,128)(2,1)S(1)} %get-tuple-element.86), channel_id=1, source_target_pairs={{0,12},{1,13},{2,14},{3,15},{4,8},{5,9},{6,10},{7,11},{8,4},{9,5},... | collective-permute-start | bytes 294920 | tf_op jit(solution)/shard_map/cond/branch_0_fun/ppermute | solution.py:78
  24.7 6.4 %collective-permute-start.7 = (bf16[3,128,128]{2,1,0:T(8,128)(2,1)S(1)}, bf16[3,128,128]{2,1,0:T(8,128)(2,1)S(1)}, u32[]{:S(2)}, u32[]{:S(2)}) collective-permute-start(bf16[3,128,128]{2,1,0:T(8,128)(2,1)S(1)} %get-tuple-element.87), channel_id=1, source_target_pairs={{0,8},{1,9},{2,10},{3,11},{4,12},{5,13},{6,14},{7,15},{8,0},{9,1},... | collective-permute-start | bytes 294920 | tf_op jit(solution)/shard_map/cond/branch_0_fun/ppermute | solution.py:78
  24.7 6.4 %collective-permute-start.8 = (bf16[3,128,128]{2,1,0:T(8,128)(2,1)S(1)}, bf16[3,128,128]{2,1,0:T(8,128)(2,1)S(1)}, u32[]{:S(2)}, u32[]{:S(2)}) collective-permute-start(bf16[3,128,128]{2,1,0:T(8,128)(2,1)S(1)} %get-tuple-element.88), channel_id=1, source_target_pairs={{0,4},{1,5},{2,6},{3,7},{4,0},{5,1},{6,2},{7,3},{8,12},{9,13},{10,... | collective-permute-start | bytes 294920 | tf_op jit(solution)/shard_map/cond/branch_0_fun/ppermute | solution.py:78
  31.1 5.3 %copy-start.8 = (f32[6,128,128]{2,1,0:T(8,128)S(1)}, f32[6,128,128]{2,1,0:T(8,128)}, u32[]{:S(2)}) copy-start(f32[6,128,128]{2,1,0:T(8,128)} %get-tuple-element.103.refs_4_.refs_2_) | copy-start | bytes 1179652 | tf_op jit(solution)/shard_map/cond
  31.1 5.3 %copy-start.11 = (f32[6,128,128]{2,1,0:T(8,128)S(1)}, f32[6,128,128]{2,1,0:T(8,128)}, u32[]{:S(2)}) copy-start(f32[6,128,128]{2,1,0:T(8,128)} %get-tuple-element.104.refs_5_.refs_3_) | copy-start | bytes 1179652 | tf_op jit(solution)/shard_map/cond
  31.9 9.7 %collective-permute-start.11 = (bf16[3,128,128]{2,1,0:T(8,128)(2,1)S(1)}, bf16[3,128,128]{2,1,0:T(8,128)(2,1)S(1)}, u32[]{:S(2)}, u32[]{:S(2)}) collective-permute-start(bf16[3,128,128]{2,1,0:T(8,128)(2,1)S(1)} %get-tuple-element.100.refs_4_), channel_id=1, source_target_pairs={{0,12},{1,13},{2,14},{3,15},{4,8},{5,9},{6,10},{7,11},{8,4},{9,5},... | collective-permute-start | bytes 294920 | tf_op jit(solution)/shard_map/cond/branch_0_fun/ppermute | solution.py:78
  33.7 7.9 %collective-permute-start.10 = (bf16[3,128,128]{2,1,0:T(8,128)(2,1)S(1)}, bf16[3,128,128]{2,1,0:T(8,128)(2,1)S(1)}, u32[]{:S(2)}, u32[]{:S(2)}) collective-permute-start(bf16[3,128,128]{2,1,0:T(8,128)(2,1)S(1)} %get-tuple-element.100.refs_4_), channel_id=1, source_target_pairs={{0,8},{1,9},{2,10},{3,11},{4,12},{5,13},{6,14},{7,15},{8,0},{9,1},... | collective-permute-start | bytes 294920 | tf_op jit(solution)/shard_map/cond/branch_0_fun/ppermute | solution.py:78
  34.3 7.3 %collective-permute-start.9 = (bf16[3,128,128]{2,1,0:T(8,128)(2,1)S(1)}, bf16[3,128,128]{2,1,0:T(8,128)(2,1)S(1)}, u32[]{:S(2)}, u32[]{:S(2)}) collective-permute-start(bf16[3,128,128]{2,1,0:T(8,128)(2,1)S(1)} %get-tuple-element.100.refs_4_), channel_id=1, source_target_pairs={{0,4},{1,5},{2,6},{3,7},{4,0},{5,1},{6,2},{7,3},{8,12},{9,13},{10,... | collective-permute-start | bytes 294920 | tf_op jit(solution)/shard_map/cond/branch_0_fun/ppermute | solution.py:78
  36.4 5.2 %collective-permute-start.12 = (bf16[3,128,128]{2,1,0:T(8,128)(2,1)S(1)}, bf16[3,128,128]{2,1,0:T(8,128)(2,1)S(1)}, u32[]{:S(2)}, u32[]{:S(2)}) collective-permute-start(bf16[3,128,128]{2,1,0:T(8,128)(2,1)S(1)} %get-tuple-element.101.refs_1_), channel_id=1, source_target_pairs={{0,16},{1,17},{2,18},{3,19},{4,20},{5,21},{6,22},{7,23},{8,24},{9,... | collective-permute-start | bytes 294920 | tf_op jit(solution)/shard_map/cond/branch_0_fun/ppermute | solution.py:78
  41.7 5.0 %collective-permute-start.17 = (bf16[4,128,128]{2,1,0:T(8,128)(2,1)S(1)}, bf16[4,128,128]{2,1,0:T(8,128)(2,1)S(1)}, u32[]{:S(2)}, u32[]{:S(2)}) collective-permute-start(bf16[4,128,128]{2,1,0:T(8,128)(2,1)S(1)} %get-tuple-element.107.refs_1_), channel_id=1, source_target_pairs={{0,16},{1,17},{2,18},{3,19},{4,20},{5,21},{6,22},{7,23},{8,24},{9,... | collective-permute-start | bytes 393224 | tf_op jit(solution)/shard_map/cond/branch_0_fun/ppermute | solution.py:78
  42.6 5.0 %collective-permute-start.15 = (bf16[4,128,128]{2,1,0:T(8,128)(2,1)S(1)}, bf16[4,128,128]{2,1,0:T(8,128)(2,1)S(1)}, u32[]{:S(2)}, u32[]{:S(2)}) collective-permute-start(bf16[4,128,128]{2,1,0:T(8,128)(2,1)S(1)} %get-tuple-element.108.refs_0_), channel_id=1, source_target_pairs={{0,2},{1,3},{2,0},{3,1},{4,6},{5,7},{6,4},{7,5},{8,10},{9,11},{10,... | collective-permute-start | bytes 393224 | tf_op jit(solution)/shard_map/cond/branch_0_fun/ppermute | solution.py:78
  42.8 9.6 %collective-permute-start.13 = (bf16[4,128,128]{2,1,0:T(8,128)(2,1)S(1)}, bf16[4,128,128]{2,1,0:T(8,128)(2,1)S(1)}, u32[]{:S(2)}, u32[]{:S(2)}) collective-permute-start(bf16[4,128,128]{2,1,0:T(8,128)(2,1)S(1)} %get-tuple-element.107.refs_1_), channel_id=1, source_target_pairs={{0,2},{1,3},{2,0},{3,1},{4,6},{5,7},{6,4},{7,5},{8,10},{9,11},{10,... | collective-permute-start | bytes 393224 | tf_op jit(solution)/shard_map/cond/branch_0_fun/ppermute | solution.py:78
  44.6 7.7 %collective-permute-start.14 = (bf16[4,128,128]{2,1,0:T(8,128)(2,1)S(1)}, bf16[4,128,128]{2,1,0:T(8,128)(2,1)S(1)}, u32[]{:S(2)}, u32[]{:S(2)}) collective-permute-start(bf16[4,128,128]{2,1,0:T(8,128)(2,1)S(1)} %get-tuple-element.108.refs_0_), channel_id=1, source_target_pairs={{0,16},{1,17},{2,18},{3,19},{4,20},{5,21},{6,22},{7,23},{8,24},{9,... | collective-permute-start | bytes 393224 | tf_op jit(solution)/shard_map/cond/branch_0_fun/ppermute | solution.py:78
  47.6 6.1 %collective-permute-start.20 = (bf16[16,128,128]{2,1,0:T(8,128)(2,1)S(1)}, bf16[16,128,128]{2,1,0:T(8,128)(2,1)S(1)}, u32[]{:S(2)}, u32[]{:S(2)}) collective-permute-start(bf16[16,128,128]{2,1,0:T(8,128)(2,1)S(1)} %get-tuple-element.110.refs_6_), channel_id=1, source_target_pairs={{0,1},{1,0},{2,3},{3,2},{4,5},{5,4},{6,7},{7,6},{8,9},{9,8},{10,11... | collective-permute-start | bytes 1572872 | tf_op jit(solution)/shard_map/cond/branch_0_fun/ppermute | solution.py:78
  47.7 5.9 %collective-permute-start.18 = (bf16[4,128,128]{2,1,0:T(8,128)(2,1)S(1)}, bf16[4,128,128]{2,1,0:T(8,128)(2,1)S(1)}, u32[]{:S(2)}, u32[]{:S(2)}) collective-permute-start(bf16[4,128,128]{2,1,0:T(8,128)(2,1)S(1)} %collective-permute-done.17.refs_3_), channel_id=1, source_target_pairs={{0,2},{1,3},{2,0},{3,1},{4,6},{5,7},{6,4},{7,5},{8,10},{9,11},{10,... | collective-permute-start | bytes 393224 | tf_op jit(solution)/shard_map/cond/branch_0_fun/ppermute | solution.py:78
  47.9 5.7 %collective-permute-start.16 = (bf16[4,128,128]{2,1,0:T(8,128)(2,1)S(1)}, bf16[4,128,128]{2,1,0:T(8,128)(2,1)S(1)}, u32[]{:S(2)}, u32[]{:S(2)}) collective-permute-start(bf16[4,128,128]{2,1,0:T(8,128)(2,1)S(1)} %collective-permute-done.15.refs_2_), channel_id=1, source_target_pairs={{0,16},{1,17},{2,18},{3,19},{4,20},{5,21},{6,22},{7,23},{8,24},{9,... | collective-permute-start | bytes 393224 | tf_op jit(solution)/shard_map/cond/branch_0_fun/ppermute | solution.py:78
  53.7 2.0 %collective-permute-start.19 = (bf16[16,128,128]{2,1,0:T(8,128)(2,1)S(1)}, bf16[16,128,128]{2,1,0:T(8,128)(2,1)S(1)}, u32[]{:S(2)}, u32[]{:S(2)}) collective-permute-start(bf16[16,128,128]{2,1,0:T(8,128)(2,1)S(1)} %get-tuple-element.113.refs_11_), channel_id=1, source_target_pairs={{0,1},{1,0},{2,3},{3,2},{4,5},{5,4},{6,7},{7,6},{8,9},{9,8},{10,11... | collective-permute-start | bytes 1572872 | tf_op jit(solution)/shard_map/cond/branch_0_fun/ppermute | solution.py:78
